TPU v7x, 32 devices: a whole 2x2x4 slice. The times are simulated.
32 devices in a mesh: groups: 2 (over x), wide: 16 (over z, y, core).
Axes of the slice: x: 2, y: 2, z: 4, core: 2. Of those that a mesh axis runs over, the one named last changes fastest.
Arguments:
- tokens: bfloat16 [512, 6144], P(('groups', 'wide')), parts along dimension 0, may hold values from -6 to 6
- target: bfloat16 [512, 6144], P(('groups', 'wide')), parts along dimension 0, may hold values from -6 to 6
- norm_gain: float32 [6144], replicated, may hold values from 0.25 to 1.75
- up_weight: bfloat16 [6144, 12288], P(None, 'wide'), may hold values from -0.078125 to 0.078125
- down_weight: bfloat16 [12288, 6144], P('wide'), may hold values from -0.0546875 to 0.0546875
- model_codes: int32 [4, 6144], P('groups'), parts along dimension 0, may hold values from 0 to 1073741823
- hidden_codes: int32 [4, 12288], P('groups', 'wide'), parts along dimension 0, may hold values from 0 to 1073741823
Outputs:
- hessian_up: bfloat16 [12288, 12288], P('groups', 'wide'), parts along dimension 0
- hessian_down: bfloat16 [24576, 6144], P(('groups', 'wide')), parts along dimension 0
- quadratic_form: float32 [2], P('groups'), parts along dimension 0
There are 2 independent parts, one for each index of `groups`. A program takes and returns all parts, laid end to end along the dimension named above; an argument that names none is the same for every part. Nothing has to cross between parts.
Inputs may be any that keep to these rules, and one draw needn't show every extreme that they name: `model_codes`: each entry holds 30 random bits. `hidden_codes`: each entry holds 30 random bits.
All inputs are finite; a program needn't handle non-finite values.
Results may differ from a plain program's by a relative error of at most 0.0076.
Values may be sent and summed in bfloat16 or wider, within the bound.
A program may use at most 192 MiB of HBM per device.

v0:
```python
import jax
import jax.numpy as jnp
from jax import lax
from jax.sharding import PartitionSpec as P

D = 6144
FF = 12288


def normalize(rows, norm_gain):
    wide_rows = rows.astype(jnp.float32)
    center = jnp.mean(wide_rows, axis=1, keepdims=True)
    spread = jnp.mean((wide_rows - center) ** 2, axis=1, keepdims=True)
    return ((wide_rows - center) * lax.rsqrt(spread + 1e-06) * norm_gain).astype(jnp.bfloat16)


def bit_parity(values):
    folded = jnp.bitwise_xor(values, jnp.right_shift(values, 16))
    folded = jnp.bitwise_xor(folded, jnp.right_shift(folded, 8))
    folded = jnp.bitwise_xor(folded, jnp.right_shift(folded, 4))
    folded = jnp.bitwise_xor(folded, jnp.right_shift(folded, 2))
    folded = jnp.bitwise_xor(folded, jnp.right_shift(folded, 1))
    return jnp.bitwise_and(folded, 1)


def probe_signs(row_codes, column_codes, factor):
    shared = jnp.bitwise_and(row_codes[:, None], column_codes[None, :])
    parity = bit_parity(shared)
    return ((1 - 2 * parity).astype(jnp.float32) * factor).astype(jnp.bfloat16)


def gelu_parts(preact):
    density = jnp.exp(-0.5 * preact * preact) * 0.3989422804014327
    cumulative = 0.5 * (1.0 + jax.scipy.special.erf(preact * 0.7071067811865476))
    return (preact * cumulative, cumulative + preact * density, density * (2.0 - preact * preact))


def contract_last(left, right):
    return lax.dot_general(
        left, right, (((1,), (1,)), ((), ())), preferred_element_type=jnp.float32
    )


def contract_first(left, right):
    return lax.dot_general(
        left, right, (((0,), (0,)), ((), ())), preferred_element_type=jnp.float32
    )


def on_device(tokens, target, norm_gain, up_weight, down_weight, model_codes, hidden_codes):
    normed = lax.all_gather(normalize(tokens, norm_gain), "wide", axis=0, tiled=True)
    total_rows = normed.shape[0]
    probe_up = probe_signs(model_codes[0], hidden_codes[0], D ** (-0.5))
    probe_down = probe_signs(hidden_codes[1], model_codes[1], FF ** (-0.5))
    preact = jnp.dot(normed, up_weight, preferred_element_type=jnp.float32)
    hidden_f32, first_slope, second_slope = gelu_parts(preact)
    hidden_act = hidden_f32.astype(jnp.bfloat16)
    forward_part = jnp.dot(hidden_act, down_weight, preferred_element_type=jnp.float32)
    tangent = jnp.dot(normed, probe_up, preferred_element_type=jnp.float32)
    hidden_tan = (first_slope * tangent).astype(jnp.bfloat16)
    tangent_part = jnp.dot(hidden_tan, down_weight, preferred_element_type=jnp.float32) + jnp.dot(
        hidden_act, probe_down, preferred_element_type=jnp.float32
    )
    outputs, doutputs = (
        lax.psum_scatter(forward_part, "wide", scatter_dimension=0, tiled=True),
        lax.psum_scatter(tangent_part, "wide", scatter_dimension=0, tiled=True),
    )
    outputs = tokens.astype(jnp.float32) + outputs
    residual_scaled = ((outputs - target.astype(jnp.float32)) / total_rows).astype(jnp.bfloat16)
    tangent_scaled = (doutputs / total_rows).astype(jnp.bfloat16)
    residual_all, tangent_all = (
        lax.all_gather(residual_scaled, "wide", axis=0, tiled=True),
        lax.all_gather(tangent_scaled, "wide", axis=0, tiled=True),
    )
    back_hidden = contract_last(residual_all, down_weight)
    dback_hidden = contract_last(tangent_all, down_weight) + contract_last(residual_all, probe_down)
    curvature = (second_slope * tangent * back_hidden + first_slope * dback_hidden).astype(
        jnp.bfloat16
    )
    hessian_f32_up = contract_first(normed, curvature)
    hessian_f32_down = contract_first(hidden_tan, residual_all) + contract_first(
        hidden_act, tangent_all
    )
    local_sum = jnp.sum(probe_up.astype(jnp.float32) * hessian_f32_up) + jnp.sum(
        probe_down.astype(jnp.float32) * hessian_f32_down
    )
    quadratic_form = lax.psum(local_sum, "wide")
    return (
        hessian_f32_up.astype(jnp.bfloat16),
        hessian_f32_down.astype(jnp.bfloat16),
        jnp.reshape(quadratic_form, (1,)),
    )


def solution(mesh):
    return jax.shard_map(
        on_device,
        mesh=mesh,
        in_specs=(
            P(("groups", "wide"), None),
            P(("groups", "wide"), None),
            P(),
            P(None, "wide"),
            P("wide", None),
            P("groups", None),
            P("groups", "wide"),
        ),
        out_specs=(P("groups", "wide"), P(("groups", "wide"), None), P("groups")),
        check_vma=False,
    )
```

profile of v0, /device:TPU:0, one launch (start us, length us, event | category | flops | bytes accessed | tf_op | source)
XLA Modules:
  0.0 433.9 jit_solution(16415018647727019609)
XLA Ops:
  7.2 0.0 all-gather.4.cloned.1.call-start
  7.2 1.1 convert_reduce_fusion
  8.3 1.2 fusion.44
  9.5 1.7 fusion.46
  11.2 0.0 all-gather.4.cloned.1.call-update
  11.3 0.0 reduce-scatter.3.cloned.1.call-start
  11.3 48.0 %all-gather.4.cloned.1.call-done = bf16[256,6144]{1,0:T(8,128)(2,1)} async-done(((bf16[16,6144]{1,0:T(8,128)(2,1)}), bf16[256,6144]{1,0:T(8,128)(2,1)}) %all-gather.4.cloned.1.call-update) | async-done | bytes 3145744 | tf_op jit(solution)/shard_map/all_gather | solution.py:51
  59.3 7.4 %fusion.83 = f32[256,768]{1,0:T(8,128)S(1)} fusion(bf16[256,6144]{1,0:T(8,128)(2,1)} %all-gather.4.cloned.1.call-done, bf16[6144,768]{1,0:T(8,128)(2,1)} %param.10), kind=kOutput, calls=%fused_computation.85 | convolution fusion | flops 2415919104 | bytes 13369344 | tf_op jit(solution)/shard_map/dot_general | solution.py:55
  66.7 4.6 %fusion.79 = f32[256,6144]{1,0:T(8,128)} fusion(bf16[768,6144]{1,0:T(8,128)(2,1)S(1)} %copy-done, f32[256,768]{1,0:T(8,128)S(1)} %fusion.83), kind=kOutput, calls=%fused_computation.83 | convolution fusion | flops 2416902144 | bytes 16515072 | tf_op jit(solution)/shard_map/dot_general | solution.py:58
  71.3 0.0 reduce-scatter.3.cloned.1.call-update
  71.3 0.2 reduce-scatter.5.cloned.1.call-start
  71.6 13.1 %fusion.16 = f32[256,768]{1,0:T(8,128)S(1)} fusion(bf16[256,6144]{1,0:T(8,128)(2,1)} %all-gather.4.cloned.1.call-done, s32[768]{0:T(1024)S(1)} %get-tuple-element.4, s32[6144]{0:T(1024)S(1)} %bitcast.23), kind=kOutput, calls=%fused_computation.27 | convolution fusion | flops 2496135168 | bytes 3959808 | tf_op jit(solution)/shard_map/dot_general | solution.py:59
  84.8 3.2 fusion.78
  88.0 14.6 %fusion.18 = f32[256,6144]{1,0:T(8,128)} fusion(f32[256,6144]{1,0:T(8,128)S(1)} %fusion.78, s32[6144]{0:T(1024)S(1)} %bitcast.25, s32[768]{0:T(1024)S(1)} %get-tuple-element.3, f32[256,768]{1,0:T(8,128)S(1)} %fusion.83), kind=kOutput, calls=%fused_computation.28 | convolution fusion | flops 2498691072 | bytes 13396992 | tf_op jit(solution)/shard_map/dot_general | solution.py:61
  102.6 0.0 reduce-scatter.5.cloned.1.call-update
  102.6 0.0 all-gather.6.cloned.1.call-start
  102.6 52.8 %reduce-scatter.3.cloned.1.call-done = f32[16,6144]{1,0:T(8,128)} async-done(((f32[256,6144]{1,0:T(8,128)}), f32[16,6144]{1,0:T(8,128)}) %reduce-scatter.3.cloned.1.call-update) | async-done | bytes 393232 | tf_op jit(solution)/shard_map/reduce_scatter | solution.py:65
  155.4 1.7 fusion.49
  157.2 0.0 all-gather.6.cloned.1.call-update
  157.2 0.0 all-gather.8.cloned.1.call-start
  157.2 87.7 %reduce-scatter.5.cloned.1.call-done = f32[16,6144]{1,0:T(8,128)} async-done(((f32[256,6144]{1,0:T(8,128)}), f32[16,6144]{1,0:T(8,128)}) %reduce-scatter.5.cloned.1.call-update) | async-done | bytes 393232 | tf_op jit(solution)/shard_map/reduce_scatter | solution.py:66
  245.0 1.7 multiply_convert_fusion.2
  246.7 0.0 all-gather.8.cloned.1.call-update
  246.7 45.5 %all-gather.6.cloned.1.call-done = bf16[256,6144]{1,0:T(8,128)(2,1)} async-done(((bf16[16,6144]{1,0:T(8,128)(2,1)}), bf16[256,6144]{1,0:T(8,128)(2,1)}) %all-gather.6.cloned.1.call-update) | async-done | bytes 3145744 | tf_op jit(solution)/shard_map/all_gather | solution.py:72
  292.2 7.5 %convolution_multiply_fusion = f32[256,768]{1,0:T(8,128)S(1)} fusion(bf16[256,6144]{1,0:T(8,128)(2,1)} %all-gather.6.cloned.1.call-done, bf16[768,6144]{1,0:T(8,128)(2,1)} %param.11, f32[256,768]{1,0:T(8,128)S(1)} %fusion.16, f32[256,768]{1,0:T(8,128)S(1)} %fusion.83), kind=kOutput, calls=%fused_computation.29 | convolution fusion | flops 2417491968 | bytes 14942208 | tf_op jit(solution)/shard_map/dot_general | solution.py:39
  299.7 8.3 %fusion.77 = f32[768,6144]{1,0:T(8,128)} fusion(bf16[256,6144]{1,0:T(8,128)(2,1)S(1)} %copy-done.2, f32[256,768]{1,0:T(8,128)S(1)} %fusion.16, f32[256,768]{1,0:T(8,128)S(1)} %fusion.83), kind=kOutput, calls=%fused_computation.81 | convolution fusion | flops 2417885184 | bytes 23592960 | tf_op jit(solution)/shard_map/dot_general | solution.py:45
  308.0 30.9 %all-gather.8.cloned.1.call-done = bf16[256,6144]{1,0:T(8,128)(2,1)} async-done(((bf16[16,6144]{1,0:T(8,128)(2,1)}), bf16[256,6144]{1,0:T(8,128)(2,1)}) %all-gather.8.cloned.1.call-update) | async-done | bytes 3145744 | tf_op jit(solution)/shard_map/all_gather | solution.py:73
  338.9 7.3 %fusion.84 = f32[256,768]{1,0:T(8,128)S(1)} fusion(bf16[256,6144]{1,0:T(8,128)(2,1)} %all-gather.8.cloned.1.call-done, bf16[768,6144]{1,0:T(8,128)(2,1)} %param.11), kind=kOutput, calls=%fused_computation.86 | convolution fusion | flops 2415919104 | bytes 13369344 | tf_op jit(solution)/shard_map/dot_general | solution.py:39
  346.2 20.6 %multiply_reduce_fusion = (f32[]{:T(128)}, bf16[768,6144]{1,0:T(8,128)(2,1)}) fusion(s32[6144]{0:T(1024)S(1)} %bitcast.26, s32[768]{0:T(1024)S(1)} %get-tuple-element.3, f32[768,6144]{1,0:T(8,128)} %fusion.77, bf16[256,6144]{1,0:T(8,128)(2,1)} %all-gather.8.cloned.1.call-done, f32[256,768]{1,0:T(8,128)S(1)} %fusion.83), kind=kOutput, calls=%fused_computation.20 | convolution fusion | flops 2520711168 | bytes 32271364 | tf_op jit(solution)/shard_map/dot_general | solution.py:45
  366.9 11.4 %fusion.30.clone.1.clone.4 = bf16[256,768]{1,0:T(8,128)(2,1)S(1)} fusion(f32[256,768]{1,0:T(8,128)S(1)} %convolution_multiply_fusion, f32[256,768]{1,0:T(8,128)S(1)} %fusion.84, bf16[256,6144]{1,0:T(8,128)(2,1)S(1)} %copy-done.3, s32[6144]{0:T(1024)S(1)} %bitcast.27, s32[768]{0:T(1024)S(1)} %get-tuple-element.3, ...), kind=kOutput, calls=%fused_computation.33.clone.clone.clone.clone.clone.1 | convolution fusion | flops 2498494464 | bytes 5925888 | tf_op jit(solution)/shard_map/dot_general | solution.py:39
  378.3 15.0 %multiply_reduce_fusion.1 = (f32[]{:T(128)}, bf16[6144,768]{1,0:T(8,128)(2,1)}) fusion(s32[768]{0:T(1024)S(1)} %get-tuple-element.4, s32[6144]{0:T(1024)S(1)} %bitcast.24, bf16[256,6144]{1,0:T(8,128)(2,1)S(1)} %copy-done.7, bf16[256,768]{1,0:T(8,128)(2,1)S(1)} %fusion.30.clone.1.clone.4), kind=kOutput, calls=%fused_computation.21 | convolution fusion | flops 2515009536 | bytes 13003780 | tf_op jit(solution)/shard_map/dot_general | solution.py:45
  394.5 32.6 %psum.7 = f32[1]{0:T(128)} all-reduce(f32[1]{0:T(128)} %bitcast.2), channel_id=1, replica_groups=mesh['groups'=2,'wide'=16] {'wide'}, use_global_device_ids=true, to_apply=%region_6.0 | all-reduce | flops 1 | bytes 8 | tf_op jit(solution)/shard_map/psum | solution.py:87
  (27 shorter events, 0.1 us)
Async XLA Ops:
  7.2 52.1 %all-gather.4.cloned.1.call-start = ((), (), s32[]{:S(2)}) async-start(), calls=%async_computation.2 | async-start | bytes 3342336 | tf_op jit(solution)/shard_map/all_gather | solution.py:51
  11.2 60.3 %copy-start.6 = (s32[2,768]{1,0:T(2,128)S(1)}, s32[2,768]{1,0:T(2,128)}, u32[]{:S(2)}) copy-start(s32[2,768]{1,0:T(2,128)} %param.13) | copy-start | bytes 18436
  11.3 60.3 %copy-start.5 = (s32[2,6144]{1,0:T(2,128)S(1)}, s32[2,6144]{1,0:T(2,128)}, u32[]{:S(2)}) copy-start(s32[2,6144]{1,0:T(2,128)} %param.12) | copy-start | bytes 147460
  11.3 144.2 %reduce-scatter.3.cloned.1.call-start = ((), (), s32[]{:S(2)}) async-start(), calls=%async_computation.3 | async-start | bytes 6684672 | tf_op jit(solution)/shard_map/reduce_scatter | solution.py:65
  59.3 7.4 %copy-start = (bf16[768,6144]{1,0:T(8,128)(2,1)S(1)}, bf16[768,6144]{1,0:T(8,128)(2,1)}, u32[]{:S(2)}) copy-start(bf16[768,6144]{1,0:T(8,128)(2,1)} %param.11) | copy-start | bytes 28311556
  71.3 13.5 %slice-start = ((s8[9437184]{0:T(1024)(128)(4,1)}), s8[1048576]{0:T(1024)(128)(4,1)S(1)}, s32[]{:S(2)}) async-start(s8[9437184]{0:T(1024)(128)(4,1)} %bitcast.21), calls=%async_computation.7 | async-start | bytes 2097152
  71.3 173.7 %reduce-scatter.5.cloned.1.call-start = ((), (), s32[]{:S(2)}) async-start(), calls=%async_computation.5 | async-start | bytes 6684672 | tf_op jit(solution)/shard_map/reduce_scatter | solution.py:66
  71.6 13.1 %slice-start.1 = ((s8[9437184]{0:T(1024)(128)(4,1)}), s8[4194304]{0:T(1024)(128)(4,1)S(1)}, s32[]{:S(2)}) async-start(s8[9437184]{0:T(1024)(128)(4,1)} %bitcast.21), calls=%async_computation.8 | async-start | bytes 8388608
  71.6 13.1 %slice-start.2 = ((s8[9437184]{0:T(1024)(128)(4,1)}), s8[4194304]{0:T(1024)(128)(4,1)S(1)}, s32[]{:S(2)}) async-start(s8[9437184]{0:T(1024)(128)(4,1)} %bitcast.21), calls=%async_computation.9 | async-start | bytes 8388608
  88.0 67.5 %copy-start.1 = (bf16[16,6144]{1,0:T(8,128)(2,1)S(1)}, bf16[16,6144]{1,0:T(8,128)(2,1)}, u32[]{:S(2)}) copy-start(bf16[16,6144]{1,0:T(8,128)(2,1)} %param.7) | copy-start | bytes 589828
  88.0 67.4 %copy-start.4 = (bf16[16,6144]{1,0:T(8,128)(2,1)S(1)}, bf16[16,6144]{1,0:T(8,128)(2,1)}, u32[]{:S(2)}) copy-start(bf16[16,6144]{1,0:T(8,128)(2,1)} %param.8) | copy-start | bytes 589828
  102.6 189.6 %all-gather.6.cloned.1.call-start = ((), (), s32[]{:S(2)}) async-start(), calls=%async_computation.4 | async-start | bytes 3342336 | tf_op jit(solution)/shard_map/all_gather | solution.py:72
  157.2 181.7 %all-gather.8.cloned.1.call-start = ((), (), s32[]{:S(2)}) async-start(), calls=%async_computation.6 | async-start | bytes 3342336 | tf_op jit(solution)/shard_map/all_gather | solution.py:73
  292.2 7.5 %copy-start.2 = (bf16[256,6144]{1,0:T(8,128)(2,1)S(1)}, bf16[256,6144]{1,0:T(8,128)(2,1)}, u32[]{:S(2)}) copy-start(bf16[256,6144]{1,0:T(8,128)(2,1)} %all-gather.6.cloned.1.call-done) | copy-start | bytes 9437188
  346.2 20.7 %copy-start.3 = (bf16[256,6144]{1,0:T(8,128)(2,1)S(1)}, bf16[256,6144]{1,0:T(8,128)(2,1)}, u32[]{:S(2)}) copy-start(bf16[256,6144]{1,0:T(8,128)(2,1)} %all-gather.6.cloned.1.call-done) | copy-start | bytes 9437188
  366.9 11.5 %copy-start.7 = (bf16[256,6144]{1,0:T(8,128)(2,1)S(1)}, bf16[256,6144]{1,0:T(8,128)(2,1)}, u32[]{:S(2)}) copy-start(bf16[256,6144]{1,0:T(8,128)(2,1)} %all-gather.4.cloned.1.call-done) | copy-start | bytes 9437188
Sparse Core Ops, SparseCore 0:
  11.4 47.8 all-gather.3
  71.4 83.9 reduce-scatter.2
  160.5 84.4 reduce-scatter.4
  247.7 44.4 all-gather.5
  294.9 43.9 all-gather.7
where the time goes:
time: 438 us; the launch traced here: 434 us
  waiting for transfers between devices  265 us (61%)
  matrix products  113 us (26%)
  blocking collectives  32.6 us (7%)
  between operations  15.4 us (4%)
  other arithmetic  7.45 us (2%)
    reduce_scatter x1, waiting for transfers between devices, on_device(): lax.psum_scatter(tangent_part, 'wide', scatter_dimension=0, tiled=True)  87.7 us
    reduce_scatter x1, waiting for transfers between devices, on_device(): lax.psum_scatter(forward_part, 'wide', scatter_dimension=0, tiled=True)  52.8 us
    all_gather x1, waiting for transfers between devices, on_device(): lax.all_gather(normalize(tokens, norm_gain), 'wide', axis=0, tiled=True)  48 us
    all_gather x1, waiting for transfers between devices, on_device(): lax.all_gather(residual_scaled, 'wide', axis=0, tiled=True)  45.5 us
    dot_general x3, matrix products, contract_first(): lax.dot_general(left, right, (((0,), (0,)), ((), ())), preferred_element_...  43.9 us
    psum x1, blocking collectives, on_device(): quadratic_form = lax.psum(local_sum, 'wide')  32.6 us
    all_gather x1, waiting for transfers between devices, on_device(): lax.all_gather(tangent_scaled, 'wide', axis=0, tiled=True)  30.9 us
    dot_general x3, matrix products, contract_last(): lax.dot_general(left, right, (((1,), (1,)), ((), ())), preferred_element_...  26.2 us
  transfers between devices with their start and end apart: 5, of which 5 were waited for; matrix products, arithmetic and copies ran while one was open for 12% of the time, Pallas kernels for 0%

commit v1 on v0

v1 whole, which is shorter than its diff:
```python
import functools

import jax
import jax.numpy as jnp
from jax import lax
from jax.sharding import PartitionSpec as P

D = 6144
FF = 12288


def normalize(rows, norm_gain):
    wide_rows = rows.astype(jnp.float32)
    center = jnp.mean(wide_rows, axis=1, keepdims=True)
    spread = jnp.mean((wide_rows - center) ** 2, axis=1, keepdims=True)
    return ((wide_rows - center) * lax.rsqrt(spread + 1e-06) * norm_gain).astype(jnp.bfloat16)


def probe_signs(row_codes, column_codes, factor):
    shared = jnp.bitwise_and(row_codes[:, None], column_codes[None, :])
    odd = jnp.bitwise_and(lax.population_count(shared), 1) == 1
    size = jnp.asarray(factor, jnp.float32)
    return jnp.where(odd, -size, size).astype(jnp.bfloat16)


def gelu_parts(preact):
    density = jnp.exp(-0.5 * preact * preact) * 0.3989422804014327
    cumulative = 0.5 * (1.0 + jax.scipy.special.erf(preact * 0.7071067811865476))
    return (preact * cumulative, cumulative + preact * density, density * (2.0 - preact * preact))


def contract_last(left, right):
    return lax.dot_general(
        left, right, (((1,), (1,)), ((), ())), preferred_element_type=jnp.float32
    )


def contract_first(left, right):
    return lax.dot_general(
        left, right, (((0,), (0,)), ((), ())), preferred_element_type=jnp.float32
    )


def swap(value, bit, size):
    pairs = [(i, i ^ (1 << bit)) for i in range(size)]
    return lax.ppermute(value, "wide", pairs)


def stage_orders(bits):
    first = list(range(bits))
    second = list(first)
    if bits > 2:
        second[1], second[2] = first[2], first[1]
    return first, second


def spread(rows, bits):
    return rows.reshape((1,) * bits + rows.shape)


def gather_stage(value, bit, bits, size):
    return lax.concatenate([value, swap(value, bit, size)], bits - 1 - bit)


def split_rows(total, bits, size):
    return total.reshape((2,) * bits + (total.shape[0] // size, total.shape[1]))


def scatter_stage(value, bit, bits, size):
    axis = bits - 1 - bit
    kept = lax.slice_in_dim(value, 0, 1, axis=axis)
    sent = lax.slice_in_dim(value, 1, 2, axis=axis).astype(jnp.bfloat16)
    return kept + swap(sent, bit, size).astype(jnp.float32)


def add_over(value, size):
    for bit in range(size.bit_length() - 1):
        value = value + swap(value, bit, size)
    return value


def on_device(
    size, tokens, target, norm_gain, up_weight, down_weight, model_codes, hidden_codes
):
    bits = size.bit_length() - 1
    orders = stage_orders(bits)
    own_rows, width = tokens.shape
    total_rows = own_rows * size

    probes = [
        lambda: probe_signs(model_codes[0], hidden_codes[0], D ** (-0.5)),
        lambda: probe_signs(hidden_codes[1], model_codes[1], FF ** (-0.5)),
    ]
    made = []
    own = normalize(tokens, norm_gain)
    halves = [spread(own[:, : width // 2], bits), spread(own[:, width // 2 :], bits)]
    for stage in reversed(range(bits)):
        if stage < 2:
            joined = lax.optimization_barrier((halves[0], halves[1], probes[stage]()))
            halves = [joined[0], joined[1]]
            made.append(joined[2])
        halves = [
            gather_stage(half, order[stage], bits, size) for half, order in zip(halves, orders)
        ]
    probe_down, probe_up = made
    normed = jnp.concatenate([half.reshape(total_rows, width // 2) for half in halves], axis=1)

    preact = jnp.dot(normed, up_weight, preferred_element_type=jnp.float32)
    hidden_f32, first_slope, second_slope = gelu_parts(preact)
    hidden_act = hidden_f32.astype(jnp.bfloat16)
    forward_part = jnp.dot(hidden_act, down_weight, preferred_element_type=jnp.float32)
    forward_sum = scatter_stage(split_rows(forward_part, bits, size), orders[0][0], bits, size)
    tangent = jnp.dot(normed, probe_up, preferred_element_type=jnp.float32)
    hidden_tan = (first_slope * tangent).astype(jnp.bfloat16)
    tangent_part = jnp.dot(
        hidden_tan, down_weight, preferred_element_type=jnp.float32
    ) + jnp.dot(hidden_act, probe_down, preferred_element_type=jnp.float32)
    forward_sum, tangent_part = lax.optimization_barrier((forward_sum, tangent_part))
    tangent_sum = scatter_stage(split_rows(tangent_part, bits, size), orders[1][0], bits, size)
    for stage in range(1, bits):
        forward_sum = scatter_stage(forward_sum, orders[0][stage], bits, size)
        tangent_sum = scatter_stage(tangent_sum, orders[1][stage], bits, size)
    outputs = tokens.astype(jnp.float32) + forward_sum.reshape(own_rows, width)
    doutputs = tangent_sum.reshape(own_rows, width)
    residual_own = ((outputs - target.astype(jnp.float32)) / total_rows).astype(jnp.bfloat16)
    tangent_own = (doutputs / total_rows).astype(jnp.bfloat16)
    residual_all, tangent_all = spread(residual_own, bits), spread(tangent_own, bits)
    for stage in reversed(range(bits)):
        residual_all = gather_stage(residual_all, orders[0][stage], bits, size)
        tangent_all = gather_stage(tangent_all, orders[1][stage], bits, size)
    scaled = lax.optimization_barrier(
        jnp.concatenate(
            [residual_all.reshape(total_rows, width), tangent_all.reshape(total_rows, width)],
            axis=0,
        )
    )
    hidden = lax.optimization_barrier(jnp.concatenate([hidden_tan, hidden_act], axis=0))

    back = contract_last(scaled, down_weight)
    back_hidden, back_tangent = back[:total_rows], back[total_rows:]
    back_probe = contract_last(scaled[:total_rows], probe_down)
    curvature = (
        second_slope * tangent * back_hidden + first_slope * (back_tangent + back_probe)
    ).astype(jnp.bfloat16)
    local_sum = jnp.sum(
        tangent * curvature.astype(jnp.float32)
        + hidden_tan.astype(jnp.float32) * (back_probe - back_tangent)
    ) + jnp.sum(doutputs * tangent_own.astype(jnp.float32))
    quadratic_form = add_over(jnp.reshape(local_sum, (1,)), size)
    hessian_f32_up = contract_first(normed, curvature)
    hessian_f32_down = contract_first(hidden, scaled)
    return (
        hessian_f32_up.astype(jnp.bfloat16),
        hessian_f32_down.astype(jnp.bfloat16),
        quadratic_form,
    )


def solution(mesh):
    return jax.shard_map(
        functools.partial(on_device, mesh.shape["wide"]),
        mesh=mesh,
        in_specs=(
            P(("groups", "wide"), None),
            P(("groups", "wide"), None),
            P(),
            P(None, "wide"),
            P("wide", None),
            P("groups", None),
            P("groups", "wide"),
        ),
        out_specs=(P("groups", "wide"), P(("groups", "wide"), None), P("groups")),
        check_vma=False,
    )
```

time: 438 us -> 226 us (0.52)
  waiting for transfers between devices: 265 us -> 107 us
  matrix products: 113 us -> 51.9 us
  blocking collectives: 32.6 us -> 0 us
  starting transfers between devices: 0.38 us -> 27.1 us
  other arithmetic: 7.45 us -> 28.5 us
  between operations: 15.4 us -> 5.74 us
  local copies, waits for them, and re-layouts: 0.12 us -> 5.82 us
    reduce_scatter x2 -> x0, waiting for transfers between devices: 141 us -> none  [the longest x1 87.7 us: on_device(): lax.psum_scatter(tangent_part, 'wide', scatter_dimension=0, tiled=True)]
    all_gather x3 -> x0, waiting for transfers between devices: 124 us -> none  [the longest x1 48 us: on_device(): lax.all_gather(normalize(tokens, norm_gain), 'wide', axis=0, tiled=True)]
    ppermute x0 -> x28, waiting for transfers between devices: none -> 107 us  [swap(): return lax.ppermute(value, 'wide', pairs)]
    psum x1 -> x0, blocking collectives: 32.6 us -> none  [on_device(): quadratic_form = lax.psum(local_sum, 'wide')]
    dot_general x3 -> x2, matrix products: 43.9 us -> 13.7 us  [contract_first(): lax.dot_general(left, right, (((0,), (0,)), ((), ())), preferred_element_...]
    ppermute x0 -> x28, starting transfers between devices: none -> 27.1 us  [swap(): return lax.ppermute(value, 'wide', pairs)]
    dot_general x3 -> x2, matrix products: 26.2 us -> 15.9 us  [contract_last(): lax.dot_general(left, right, (((1,), (1,)), ((), ())), preferred_element_...]
    dot_general x1, matrix products: 14.6 us -> 4.51 us  [on_device(): jnp.dot(hidden_act, probe_down, preferred_element_type=jnp.float32)]
  transfers between devices with their start and end apart: 5 -> 28, of which waited for: 5 -> 23; matrix products, arithmetic and copies ran while one was open for 12% -> 11% of each run, Pallas kernels for 0% -> 0%
where the time goes in v1:
time: 226 us
  waiting for transfers between devices  107 us (47%)
  matrix products  51.9 us (23%)
  other arithmetic  28.5 us (13%)
  starting transfers between devices  27.1 us (12%)
  local copies, waits for them, and re-layouts  5.82 us (3%)
  between operations  5.74 us (3%)
    ppermute x28, waiting for transfers between devices, swap(): return lax.ppermute(value, 'wide', pairs)  107 us
    ppermute x28, starting transfers between devices, swap(): return lax.ppermute(value, 'wide', pairs)  27.1 us
    dot_general x2, matrix products, contract_last(): lax.dot_general(left, right, (((1,), (1,)), ((), ())), preferred_element_...  15.9 us
    dot_general x2, matrix products, contract_first(): lax.dot_general(left, right, (((0,), (0,)), ((), ())), preferred_element_...  13.7 us
    convert_element_type x2, other arithmetic, probe_signs(): return jnp.where(odd, -size, size).astype(jnp.bfloat16)  11.5 us
    dot_general x1, matrix products, on_device(): preact = jnp.dot(normed, up_weight, preferred_element_type=jnp.float32)  6.91 us
    concatenate x1, other arithmetic, on_device(): jnp.concatenate([residual_all.reshape(total_rows, width), tangent_all.res...  5.28 us
    dot_general x1, matrix products, on_device(): jnp.dot(hidden_act, down_weight, preferred_element_type=jnp.float32)  4.65 us
  transfers between devices with their start and end apart: 28, of which 23 were waited for; matrix products, arithmetic and copies ran while one was open for 11% of the time, Pallas kernels for 0%

profile of v1, /device:TPU:0, one launch (start us, length us, event | category | flops | bytes accessed | tf_op | source)
XLA Modules:
  0.0 225.9 jit_solution(5272167527107082272)
XLA Ops:
  4.0 4.1 %collective-permute-start = (bf16[1,1,1,1,16,3072]{5,4,3,2,1,0:T(8,128)(2,1)S(1)}, bf16[1,1,1,1,16,3072]{5,4,3,2,1,0:T(8,128)(2,1)S(1)}, u32[]{:S(2)}, u32[]{:S(2)}) collective-permute-start(bf16[1,1,1,1,16,3072]{5,4,3,2,1,0:T(8,128)(2,1)S(1)} %get-tuple-element.26), channel_id=1, source_target_pairs={{0,8},{1,9},{2,10},{3,11},{4,12},{5,13},{6,14},{7,15},{8,0},{9,1},... | collective-permute-start | bytes 294920 | tf_op jit(solution)/shard_map/ppermute | solution.py:46
  9.9 7.4 %select_convert_fusion.1 = bf16[768,6144]{1,0:T(8,128)(2,1)} fusion(s32[6144]{0:T(1024)S(1)} %bitcast.61, s32[768]{0:T(1024)S(1)} %get-tuple-element.20), kind=kLoop, calls=%fused_computation.2 | loop fusion | flops 28311552 | bytes 9464832 | tf_op jit(solution)/shard_map/convert_element_type | solution.py:23
  20.8 2.9 %collective-permute-done.1 = bf16[2,1,1,1,16,3072]{5,4,3,2,1,0:T(8,128)(2,1)S(1)} collective-permute-done((bf16[2,1,1,1,16,3072]{5,4,3,2,1,0:T(8,128)(2,1)S(1)}, bf16[2,1,1,1,16,3072]{5,4,3,2,1,0:T(8,128)(2,1)S(1)}, u32[]{:S(2)}, u32[]{:S(2)}) %collective-permute-start.1) | collective-permute-done | bytes 196640 | tf_op jit(solution)/shard_map/ppermute | solution.py:46
  27.2 4.2 %select_convert_fusion = bf16[6144,768]{1,0:T(8,128)(2,1)S(1)} fusion(s32[768]{0:T(1024)S(1)} %get-tuple-element.19, s32[6144]{0:T(1024)S(1)} %bitcast.60), kind=kLoop, calls=%fused_computation | loop fusion | flops 28311552 | bytes 9464832 | tf_op jit(solution)/shard_map/convert_element_type | solution.py:23
  31.3 3.0 %collective-permute-done.4 = bf16[2,2,1,1,16,3072]{5,4,3,2,1,0:T(8,128)(2,1)S(1)} collective-permute-done((bf16[2,2,1,1,16,3072]{5,4,3,2,1,0:T(8,128)(2,1)S(1)}, bf16[2,2,1,1,16,3072]{5,4,3,2,1,0:T(8,128)(2,1)S(1)}, u32[]{:S(2)}, u32[]{:S(2)}) %collective-permute-start.4) | collective-permute-done | bytes 393248 | tf_op jit(solution)/shard_map/ppermute | solution.py:46
  39.3 6.9 %fusion.3 = f32[256,768]{1,0:T(8,128)S(1)} fusion(bf16[6144,768]{1,0:T(8,128)(2,1)} %param.10, bf16[256,3072]{1,0:T(8,128)(2,1)S(1)} %bitcast.54, bf16[256,3072]{1,0:T(8,128)(2,1)S(1)} %bitcast.57), kind=kOutput, calls=%fused_computation.27 | convolution fusion | flops 2422210560 | bytes 13369344 | tf_op jit(solution)/shard_map/dot_general | solution.py:108
  46.3 3.6 %multiply_convert_fusion = (bf16[256,768]{1,0:T(8,128)(2,1)S(1)}, bf16[256,768]{1,0:T(8,128)(2,1)S(1)}, f32[256,768]{1,0:T(8,128)}) fusion(f32[256,768]{1,0:T(8,128)S(1)} %fusion.3, bf16[6144,768]{1,0:T(8,128)(2,1)S(1)} %select_convert_fusion, bf16[256,3072]{1,0:T(8,128)(2,1)S(1)} %bitcast.55, bf16[256,3072]{1,0:T(8,128)(2,1)S(1)} %bitcast.58), kind=kOutput, calls=%fused_computation.47 | convolution fusion | flops 2424569856 | bytes 14942208 | tf_op jit(solution)/shard_map/dot_general | solution.py:113
  49.9 4.6 %fusion.30 = f32[256,6144]{1,0:T(8,128)} fusion(bf16[256,768]{1,0:T(8,128)(2,1)S(1)} %get-tuple-element.24, bf16[768,6144]{1,0:T(8,128)(2,1)S(1)} %bitcast.45), kind=kOutput, calls=%fused_computation.88 | convolution fusion | flops 2415919104 | bytes 16121856 | tf_op jit(solution)/shard_map/dot_general | solution.py:111
  54.5 2.2 slice.164
  57.0 2.6 %fusion.31 = f32[256,6144]{1,0:T(8,128)S(1)} fusion(bf16[256,768]{1,0:T(8,128)(2,1)S(1)} %get-tuple-element.23, bf16[768,6144]{1,0:T(8,128)(2,1)S(1)} %bitcast.45), kind=kOutput, calls=%fused_computation.89 | convolution fusion | flops 2415919104 | bytes 16121856 | tf_op jit(solution)/shard_map/dot_general | solution.py:115
  59.6 4.5 %convolution_add_fusion = f32[256,6144]{1,0:T(8,128)} fusion(f32[256,6144]{1,0:T(8,128)S(1)} %fusion.31, bf16[256,768]{1,0:T(8,128)(2,1)S(1)} %get-tuple-element.24, bf16[768,6144]{1,0:T(8,128)(2,1)S(1)} %bitcast.47), kind=kOutput, calls=%fused_computation.6 | convolution fusion | flops 2417491968 | bytes 22413312 | tf_op jit(solution)/shard_map/dot_general | solution.py:117
  64.1 2.4 %slice_add_fusion.1 = f32[2,2,2,1,16,6144]{5,4,3,2,1,0:T(8,128)S(1)} fusion(f32[2,2,2,2,16,6144]{5,4,3,2,1,0:T(8,128)} %bitcast.6, bf16[2,2,2,1,16,6144]{5,4,3,2,1,0:T(8,128)(2,1)S(1)} %collective-permute-done.8), kind=kLoop, calls=%fused_computation.13 | loop fusion | flops 1572864 | bytes 7864320 | tf_op jit(solution)/shard_map/add | solution.py:73
  69.1 2.4 %collective-permute-done.16 = bf16[2,2,2,1,16,6144]{5,4,3,2,1,0:T(8,128)(2,1)S(1)} collective-permute-done((bf16[2,2,2,1,16,6144]{5,4,3,2,1,0:T(8,128)(2,1)S(1)}, bf16[2,2,2,1,16,6144]{5,4,3,2,1,0:T(8,128)(2,1)S(1)}, u32[]{:S(2)}, u32[]{:S(2)}) %collective-permute-start.16) | collective-permute-done | bytes 1572896 | tf_op jit(solution)/shard_map/ppermute | solution.py:46
  72.5 15.7 %collective-permute-done.9 = bf16[2,2,1,1,16,6144]{5,4,3,2,1,0:T(8,128)(2,1)S(1)} collective-permute-done((bf16[2,2,1,1,16,6144]{5,4,3,2,1,0:T(8,128)(2,1)S(1)}, bf16[2,2,1,1,16,6144]{5,4,3,2,1,0:T(8,128)(2,1)S(1)}, u32[]{:S(2)}, u32[]{:S(2)}) %collective-permute-start.9) | collective-permute-done | bytes 786464 | tf_op jit(solution)/shard_map/ppermute | solution.py:46
  89.0 3.3 %collective-permute-done.17 = bf16[2,1,2,1,16,6144]{5,4,3,2,1,0:T(8,128)(2,1)S(1)} collective-permute-done((bf16[2,1,2,1,16,6144]{5,4,3,2,1,0:T(8,128)(2,1)S(1)}, bf16[2,1,2,1,16,6144]{5,4,3,2,1,0:T(8,128)(2,1)S(1)}, u32[]{:S(2)}, u32[]{:S(2)}) %collective-permute-start.17) | collective-permute-done | bytes 786464 | tf_op jit(solution)/shard_map/ppermute | solution.py:46
  93.2 7.0 %collective-permute-done.10 = bf16[2,1,1,1,16,6144]{5,4,3,2,1,0:T(8,128)(2,1)S(1)} collective-permute-done((bf16[2,1,1,1,16,6144]{5,4,3,2,1,0:T(8,128)(2,1)S(1)}, bf16[2,1,1,1,16,6144]{5,4,3,2,1,0:T(8,128)(2,1)S(1)}, u32[]{:S(2)}, u32[]{:S(2)}) %collective-permute-start.10) | collective-permute-done | bytes 393248 | tf_op jit(solution)/shard_map/ppermute | solution.py:46
  100.4 2.6 %collective-permute-start.11 = (bf16[1,1,1,1,16,6144]{5,4,3,2,1,0:T(8,128)(2,1)S(1)}, bf16[1,1,1,1,16,6144]{5,4,3,2,1,0:T(8,128)(2,1)S(1)}, u32[]{:S(2)}, u32[]{:S(2)}) collective-permute-start(bf16[1,1,1,1,16,6144]{5,4,3,2,1,0:T(8,128)(2,1)S(1)} %slice.170), channel_id=1, source_target_pairs={{0,8},{1,9},{2,10},{3,11},{4,12},{5,13},{6,14},{7,15},{8,0},{9,1},... | collective-permute-start | bytes 589832 | tf_op jit(solution)/shard_map/ppermute | solution.py:46
  103.1 2.3 %collective-permute-start.19 = (bf16[1,1,1,1,16,6144]{5,4,3,2,1,0:T(8,128)(2,1)S(1)}, bf16[1,1,1,1,16,6144]{5,4,3,2,1,0:T(8,128)(2,1)S(1)}, u32[]{:S(2)}, u32[]{:S(2)}) collective-permute-start(bf16[1,1,1,1,16,6144]{5,4,3,2,1,0:T(8,128)(2,1)S(1)} %slice.169), channel_id=1, source_target_pairs={{0,8},{1,9},{2,10},{3,11},{4,12},{5,13},{6,14},{7,15},{8,0},{9,1},... | collective-permute-start | bytes 589832 | tf_op jit(solution)/shard_map/ppermute | solution.py:46
  105.4 10.8 %collective-permute-done.11 = bf16[1,1,1,1,16,6144]{5,4,3,2,1,0:T(8,128)(2,1)S(1)} collective-permute-done((bf16[1,1,1,1,16,6144]{5,4,3,2,1,0:T(8,128)(2,1)S(1)}, bf16[1,1,1,1,16,6144]{5,4,3,2,1,0:T(8,128)(2,1)S(1)}, u32[]{:S(2)}, u32[]{:S(2)}) %collective-permute-start.11) | collective-permute-done | bytes 196640 | tf_op jit(solution)/shard_map/ppermute | solution.py:46
  116.4 8.2 %collective-permute-done.19 = bf16[1,1,1,1,16,6144]{5,4,3,2,1,0:T(8,128)(2,1)S(1)} collective-permute-done((bf16[1,1,1,1,16,6144]{5,4,3,2,1,0:T(8,128)(2,1)S(1)}, bf16[1,1,1,1,16,6144]{5,4,3,2,1,0:T(8,128)(2,1)S(1)}, u32[]{:S(2)}, u32[]{:S(2)}) %collective-permute-start.19) | collective-permute-done | bytes 196640 | tf_op jit(solution)/shard_map/ppermute | solution.py:46
  124.8 8.3 %collective-permute-done.12 = bf16[1,1,1,1,16,6144]{5,4,3,2,1,0:T(8,128)(2,1)S(1)} collective-permute-done((bf16[1,1,1,1,16,6144]{5,4,3,2,1,0:T(8,128)(2,1)S(1)}, bf16[1,1,1,1,16,6144]{5,4,3,2,1,0:T(8,128)(2,1)S(1)}, u32[]{:S(2)}, u32[]{:S(2)}) %collective-permute-start.12) | collective-permute-done | bytes 196640 | tf_op jit(solution)/shard_map/ppermute | solution.py:46
  133.9 3.4 %collective-permute-done.20 = bf16[1,1,1,1,16,6144]{5,4,3,2,1,0:T(8,128)(2,1)S(1)} collective-permute-done((bf16[1,1,1,1,16,6144]{5,4,3,2,1,0:T(8,128)(2,1)S(1)}, bf16[1,1,1,1,16,6144]{5,4,3,2,1,0:T(8,128)(2,1)S(1)}, u32[]{:S(2)}, u32[]{:S(2)}) %collective-permute-start.20) | collective-permute-done | bytes 196640 | tf_op jit(solution)/shard_map/ppermute | solution.py:46
  137.9 7.7 %collective-permute-done.13 = bf16[2,1,1,1,16,6144]{5,4,3,2,1,0:T(8,128)(2,1)S(1)} collective-permute-done((bf16[2,1,1,1,16,6144]{5,4,3,2,1,0:T(8,128)(2,1)S(1)}, bf16[2,1,1,1,16,6144]{5,4,3,2,1,0:T(8,128)(2,1)S(1)}, u32[]{:S(2)}, u32[]{:S(2)}) %collective-permute-start.13) | collective-permute-done | bytes 393248 | tf_op jit(solution)/shard_map/ppermute | solution.py:46
  148.5 16.7 %collective-permute-done.14 = bf16[2,2,1,1,16,6144]{5,4,3,2,1,0:T(8,128)(2,1)S(1)} collective-permute-done((bf16[2,2,1,1,16,6144]{5,4,3,2,1,0:T(8,128)(2,1)S(1)}, bf16[2,2,1,1,16,6144]{5,4,3,2,1,0:T(8,128)(2,1)S(1)}, u32[]{:S(2)}, u32[]{:S(2)}) %collective-permute-start.14) | collective-permute-done | bytes 786464 | tf_op jit(solution)/shard_map/ppermute | solution.py:46
  172.9 5.3 %pad_maximum_fusion = bf16[512,6144]{1,0:T(8,128)(2,1)} fusion(bf16[256,6144]{1,0:T(8,128)(2,1)} %bitcast.51, bf16[256,6144]{1,0:T(8,128)(2,1)S(1)} %bitcast.50), kind=kLoop, calls=%fused_computation.7 | loop fusion | flops 12582912 | bytes 12582912 | tf_op jit(solution)/shard_map/concatenate | solution.py:132
  178.2 7.3 %fusion.32 = f32[512,768]{1,0:T(8,128)S(1)} fusion(bf16[512,6144]{1,0:T(8,128)(2,1)} %pad_maximum_fusion, bf16[768,6144]{1,0:T(8,128)(2,1)S(1)} %bitcast.45), kind=kOutput, calls=%fused_computation.90 | convolution fusion | flops 4831838208 | bytes 17301504 | tf_op jit(solution)/shard_map/dot_general | solution.py:33
  185.6 8.5 %add_reduce_fusion = (f32[]{:T(128)}, bf16[256,768]{1,0:T(8,128)(2,1)S(1)}) fusion(bf16[256,768]{1,0:T(8,128)(2,1)S(1)} %get-tuple-element.23, f32[256,768]{1,0:T(8,128)S(1)} %copy-done.10, f32[512,768]{1,0:T(8,128)S(1)} %fusion.32, f32[256,768]{1,0:T(8,128)S(1)} %copy-done.9, bf16[768,6144]{1,0:T(8,128)(2,1)} %select_convert_fusion.1, ...), kind=kOutput, calls=%fused_computation.46 | convolution fusion | flops 2420637696 | bytes 16515076 | tf_op jit(solution)/shard_map/dot_general | solution.py:33
  194.2 5.9 %convolution_convert_fusion = bf16[6144,768]{1,0:T(8,128)(2,1)} fusion(bf16[256,768]{1,0:T(8,128)(2,1)S(1)} %get-tuple-element.22, bf16[256,3072]{1,0:T(8,128)(2,1)S(1)} %bitcast.56, bf16[256,3072]{1,0:T(8,128)(2,1)S(1)} %bitcast.59), kind=kOutput, calls=%fused_computation.4 | convolution fusion | flops 2426929152 | bytes 12976128 | tf_op jit(solution)/shard_map/dot_general | solution.py:39
  200.1 7.9 %convolution_convert_fusion.1 = bf16[768,6144]{1,0:T(8,128)(2,1)} fusion(bf16[512,768]{1,0:T(8,128)(2,1)S(1)} %copy-done.6, bf16[512,6144]{1,0:T(8,128)(2,1)S(1)} %bitcast.53), kind=kOutput, calls=%fused_computation.5 | convolution fusion | flops 4836556800 | bytes 16515072 | tf_op jit(solution)/shard_map/dot_general | solution.py:39
  216.7 2.3 %collective-permute-done.26 = f32[1]{0:T(128)} collective-permute-done((f32[1]{0:T(128)}, f32[1]{0:T(128)}, u32[]{:S(2)}, u32[]{:S(2)}) %collective-permute-start.26) | collective-permute-done | bytes 36 | tf_op jit(solution)/shard_map/ppermute | solution.py:46
  219.6 2.2 collective-permute-start.27
  221.8 2.4 %collective-permute-done.27 = f32[1]{0:T(128)} collective-permute-done((f32[1]{0:T(128)}, f32[1]{0:T(128)}, u32[]{:S(2)}, u32[]{:S(2)}) %collective-permute-start.27) | collective-permute-done | bytes 36 | tf_op jit(solution)/shard_map/ppermute | solution.py:46
  (119 shorter events, 41.4 us)
Async XLA Ops:
  4.0 13.3 %collective-permute-start = (bf16[1,1,1,1,16,3072]{5,4,3,2,1,0:T(8,128)(2,1)S(1)}, bf16[1,1,1,1,16,3072]{5,4,3,2,1,0:T(8,128)(2,1)S(1)}, u32[]{:S(2)}, u32[]{:S(2)}) collective-permute-start(bf16[1,1,1,1,16,3072]{5,4,3,2,1,0:T(8,128)(2,1)S(1)} %get-tuple-element.26), channel_id=1, source_target_pairs={{0,8},{1,9},{2,10},{3,11},{4,12},{5,13},{6,14},{7,15},{8,0},{9,1},... | collective-permute-start | bytes 294920 | tf_op jit(solution)/shard_map/ppermute | solution.py:46
  8.1 11.1 %collective-permute-start.2 = (bf16[1,1,1,1,16,3072]{5,4,3,2,1,0:T(8,128)(2,1)S(1)}, bf16[1,1,1,1,16,3072]{5,4,3,2,1,0:T(8,128)(2,1)S(1)}, u32[]{:S(2)}, u32[]{:S(2)}) collective-permute-start(bf16[1,1,1,1,16,3072]{5,4,3,2,1,0:T(8,128)(2,1)S(1)} %get-tuple-element.25), channel_id=1, source_target_pairs={{0,8},{1,9},{2,10},{3,11},{4,12},{5,13},{6,14},{7,15},{8,0},{9,1},... | collective-permute-start | bytes 294920 | tf_op jit(solution)/shard_map/ppermute | solution.py:46
  17.3 6.4 %collective-permute-start.1 = (bf16[2,1,1,1,16,3072]{5,4,3,2,1,0:T(8,128)(2,1)S(1)}, bf16[2,1,1,1,16,3072]{5,4,3,2,1,0:T(8,128)(2,1)S(1)}, u32[]{:S(2)}, u32[]{:S(2)}) collective-permute-start(bf16[2,1,1,1,16,3072]{5,4,3,2,1,0:T(8,128)(2,1)S(1)} %pad_maximum_fusion.20), channel_id=1, source_target_pairs={{0,4},{1,5},{2,6},{3,7},{4,0},{5,1},{6,2},{7,3},{8,12},{9,13},{10,... | collective-permute-start | bytes 589832 | tf_op jit(solution)/shard_map/ppermute | solution.py:46
  19.2 5.9 %collective-permute-start.3 = (bf16[2,1,1,1,16,3072]{5,4,3,2,1,0:T(8,128)(2,1)S(1)}, bf16[2,1,1,1,16,3072]{5,4,3,2,1,0:T(8,128)(2,1)S(1)}, u32[]{:S(2)}, u32[]{:S(2)}) collective-permute-start(bf16[2,1,1,1,16,3072]{5,4,3,2,1,0:T(8,128)(2,1)S(1)} %pad_maximum_fusion.21), channel_id=1, source_target_pairs={{0,2},{1,3},{2,0},{3,1},{4,6},{5,7},{6,4},{7,5},{8,10},{9,11},{10,... | collective-permute-start | bytes 589832 | tf_op jit(solution)/shard_map/ppermute | solution.py:46
  25.1 9.2 %collective-permute-start.4 = (bf16[2,2,1,1,16,3072]{5,4,3,2,1,0:T(8,128)(2,1)S(1)}, bf16[2,2,1,1,16,3072]{5,4,3,2,1,0:T(8,128)(2,1)S(1)}, u32[]{:S(2)}, u32[]{:S(2)}) collective-permute-start(bf16[2,2,1,1,16,3072]{5,4,3,2,1,0:T(8,128)(2,1)S(1)} %pad_maximum_fusion.16), channel_id=1, source_target_pairs={{0,2},{1,3},{2,0},{3,1},{4,6},{5,7},{6,4},{7,5},{8,10},{9,11},{10,... | collective-permute-start | bytes 1179656 | tf_op jit(solution)/shard_map/ppermute | solution.py:46
  26.7 8.8 %collective-permute-start.5 = (bf16[2,1,2,1,16,3072]{5,4,3,2,1,0:T(8,128)(2,1)S(1)}, bf16[2,1,2,1,16,3072]{5,4,3,2,1,0:T(8,128)(2,1)S(1)}, u32[]{:S(2)}, u32[]{:S(2)}) collective-permute-start(bf16[2,1,2,1,16,3072]{5,4,3,2,1,0:T(8,128)(2,1)S(1)} %pad_maximum_fusion.17), channel_id=1, source_target_pairs={{0,4},{1,5},{2,6},{3,7},{4,0},{5,1},{6,2},{7,3},{8,12},{9,13},{10,... | collective-permute-start | bytes 1179656 | tf_op jit(solution)/shard_map/ppermute | solution.py:46
  35.6 2.4 %collective-permute-start.7 = (bf16[2,2,2,1,16,3072]{5,4,3,2,1,0:T(8,128)(2,1)S(1)}, bf16[2,2,2,1,16,3072]{5,4,3,2,1,0:T(8,128)(2,1)S(1)}, u32[]{:S(2)}, u32[]{:S(2)}) collective-permute-start(bf16[2,2,2,1,16,3072]{5,4,3,2,1,0:T(8,128)(2,1)S(1)} %pad_maximum_fusion.12), channel_id=1, source_target_pairs={{0,1},{1,0},{2,3},{3,2},{4,5},{5,4},{6,7},{7,6},{8,9},{9,8},{10,11... | collective-permute-start | bytes 2359304 | tf_op jit(solution)/shard_map/ppermute | solution.py:46
  35.7 3.4 %collective-permute-start.6 = (bf16[2,2,2,1,16,3072]{5,4,3,2,1,0:T(8,128)(2,1)S(1)}, bf16[2,2,2,1,16,3072]{5,4,3,2,1,0:T(8,128)(2,1)S(1)}, u32[]{:S(2)}, u32[]{:S(2)}) collective-permute-start(bf16[2,2,2,1,16,3072]{5,4,3,2,1,0:T(8,128)(2,1)S(1)} %pad_maximum_fusion.11), channel_id=1, source_target_pairs={{0,1},{1,0},{2,3},{3,2},{4,5},{5,4},{6,7},{7,6},{8,9},{9,8},{10,11... | collective-permute-start | bytes 2359304 | tf_op jit(solution)/shard_map/ppermute | solution.py:46
  56.7 7.4 %collective-permute-start.8 = (bf16[2,2,2,1,16,6144]{5,4,3,2,1,0:T(8,128)(2,1)S(1)}, bf16[2,2,2,1,16,6144]{5,4,3,2,1,0:T(8,128)(2,1)S(1)}, u32[]{:S(2)}, u32[]{:S(2)}) collective-permute-start(bf16[2,2,2,1,16,6144]{5,4,3,2,1,0:T(8,128)(2,1)S(1)} %slice.164), channel_id=1, source_target_pairs={{0,1},{1,0},{2,3},{3,2},{4,5},{5,4},{6,7},{7,6},{8,9},{9,8},{10,11... | collective-permute-start | bytes 4718600 | tf_op jit(solution)/shard_map/ppermute | solution.py:46
  68.0 3.5 %collective-permute-start.16 = (bf16[2,2,2,1,16,6144]{5,4,3,2,1,0:T(8,128)(2,1)S(1)}, bf16[2,2,2,1,16,6144]{5,4,3,2,1,0:T(8,128)(2,1)S(1)}, u32[]{:S(2)}, u32[]{:S(2)}) collective-permute-start(bf16[2,2,2,1,16,6144]{5,4,3,2,1,0:T(8,128)(2,1)S(1)} %slice.163), channel_id=1, source_target_pairs={{0,1},{1,0},{2,3},{3,2},{4,5},{5,4},{6,7},{7,6},{8,9},{9,8},{10,11... | collective-permute-start | bytes 4718600 | tf_op jit(solution)/shard_map/ppermute | solution.py:46
  68.6 19.6 %collective-permute-start.9 = (bf16[2,2,1,1,16,6144]{5,4,3,2,1,0:T(8,128)(2,1)S(1)}, bf16[2,2,1,1,16,6144]{5,4,3,2,1,0:T(8,128)(2,1)S(1)}, u32[]{:S(2)}, u32[]{:S(2)}) collective-permute-start(bf16[2,2,1,1,16,6144]{5,4,3,2,1,0:T(8,128)(2,1)S(1)} %slice.166), channel_id=1, source_target_pairs={{0,2},{1,3},{2,0},{3,1},{4,6},{5,7},{6,4},{7,5},{8,10},{9,11},{10,... | collective-permute-start | bytes 2359304 | tf_op jit(solution)/shard_map/ppermute | solution.py:46
  71.9 20.4 %collective-permute-start.17 = (bf16[2,1,2,1,16,6144]{5,4,3,2,1,0:T(8,128)(2,1)S(1)}, bf16[2,1,2,1,16,6144]{5,4,3,2,1,0:T(8,128)(2,1)S(1)}, u32[]{:S(2)}, u32[]{:S(2)}) collective-permute-start(bf16[2,1,2,1,16,6144]{5,4,3,2,1,0:T(8,128)(2,1)S(1)} %slice.165), channel_id=1, source_target_pairs={{0,4},{1,5},{2,6},{3,7},{4,0},{5,1},{6,2},{7,3},{8,12},{9,13},{10,... | collective-permute-start | bytes 2359304 | tf_op jit(solution)/shard_map/ppermute | solution.py:46
  88.4 11.8 %collective-permute-start.10 = (bf16[2,1,1,1,16,6144]{5,4,3,2,1,0:T(8,128)(2,1)S(1)}, bf16[2,1,1,1,16,6144]{5,4,3,2,1,0:T(8,128)(2,1)S(1)}, u32[]{:S(2)}, u32[]{:S(2)}) collective-permute-start(bf16[2,1,1,1,16,6144]{5,4,3,2,1,0:T(8,128)(2,1)S(1)} %slice.168), channel_id=1, source_target_pairs={{0,4},{1,5},{2,6},{3,7},{4,0},{5,1},{6,2},{7,3},{8,12},{9,13},{10,... | collective-permute-start | bytes 1179656 | tf_op jit(solution)/shard_map/ppermute | solution.py:46
  92.5 23.7 %copy-start.1 = (bf16[16,6144]{1,0:T(8,128)(2,1)S(1)}, bf16[16,6144]{1,0:T(8,128)(2,1)}, u32[]{:S(2)}) copy-start(bf16[16,6144]{1,0:T(8,128)(2,1)} %param.7) | copy-start | bytes 589828
  92.6 23.7 %copy-start.7 = (bf16[16,6144]{1,0:T(8,128)(2,1)S(1)}, bf16[16,6144]{1,0:T(8,128)(2,1)}, u32[]{:S(2)}) copy-start(bf16[16,6144]{1,0:T(8,128)(2,1)} %param.8) | copy-start | bytes 589828
  92.6 10.4 %collective-permute-start.18 = (bf16[2,1,1,1,16,6144]{5,4,3,2,1,0:T(8,128)(2,1)S(1)}, bf16[2,1,1,1,16,6144]{5,4,3,2,1,0:T(8,128)(2,1)S(1)}, u32[]{:S(2)}, u32[]{:S(2)}) collective-permute-start(bf16[2,1,1,1,16,6144]{5,4,3,2,1,0:T(8,128)(2,1)S(1)} %slice.167), channel_id=1, source_target_pairs={{0,2},{1,3},{2,0},{3,1},{4,6},{5,7},{6,4},{7,5},{8,10},{9,11},{10,... | collective-permute-start | bytes 1179656 | tf_op jit(solution)/shard_map/ppermute | solution.py:46
  100.4 15.9 %collective-permute-start.11 = (bf16[1,1,1,1,16,6144]{5,4,3,2,1,0:T(8,128)(2,1)S(1)}, bf16[1,1,1,1,16,6144]{5,4,3,2,1,0:T(8,128)(2,1)S(1)}, u32[]{:S(2)}, u32[]{:S(2)}) collective-permute-start(bf16[1,1,1,1,16,6144]{5,4,3,2,1,0:T(8,128)(2,1)S(1)} %slice.170), channel_id=1, source_target_pairs={{0,8},{1,9},{2,10},{3,11},{4,12},{5,13},{6,14},{7,15},{8,0},{9,1},... | collective-permute-start | bytes 589832 | tf_op jit(solution)/shard_map/ppermute | solution.py:46
  103.1 21.5 %collective-permute-start.19 = (bf16[1,1,1,1,16,6144]{5,4,3,2,1,0:T(8,128)(2,1)S(1)}, bf16[1,1,1,1,16,6144]{5,4,3,2,1,0:T(8,128)(2,1)S(1)}, u32[]{:S(2)}, u32[]{:S(2)}) collective-permute-start(bf16[1,1,1,1,16,6144]{5,4,3,2,1,0:T(8,128)(2,1)S(1)} %slice.169), channel_id=1, source_target_pairs={{0,8},{1,9},{2,10},{3,11},{4,12},{5,13},{6,14},{7,15},{8,0},{9,1},... | collective-permute-start | bytes 589832 | tf_op jit(solution)/shard_map/ppermute | solution.py:46
  116.3 16.7 %collective-permute-start.12 = (bf16[1,1,1,1,16,6144]{5,4,3,2,1,0:T(8,128)(2,1)S(1)}, bf16[1,1,1,1,16,6144]{5,4,3,2,1,0:T(8,128)(2,1)S(1)}, u32[]{:S(2)}, u32[]{:S(2)}) collective-permute-start(bf16[1,1,1,1,16,6144]{5,4,3,2,1,0:T(8,128)(2,1)S(1)} %fusion.24), channel_id=1, source_target_pairs={{0,8},{1,9},{2,10},{3,11},{4,12},{5,13},{6,14},{7,15},{8,0},{9,1},... | collective-permute-start | bytes 589832 | tf_op jit(solution)/shard_map/ppermute | solution.py:46
  124.7 12.6 %collective-permute-start.20 = (bf16[1,1,1,1,16,6144]{5,4,3,2,1,0:T(8,128)(2,1)S(1)}, bf16[1,1,1,1,16,6144]{5,4,3,2,1,0:T(8,128)(2,1)S(1)}, u32[]{:S(2)}, u32[]{:S(2)}) collective-permute-start(bf16[1,1,1,1,16,6144]{5,4,3,2,1,0:T(8,128)(2,1)S(1)} %multiply_convert_fusion.2), channel_id=1, source_target_pairs={{0,8},{1,9},{2,10},{3,11},{4,12},{5,13},{6,14},{7,15},{8,0},{9,1},... | collective-permute-start | bytes 589832 | tf_op jit(solution)/shard_map/ppermute | solution.py:46
  133.1 12.5 %collective-permute-start.13 = (bf16[2,1,1,1,16,6144]{5,4,3,2,1,0:T(8,128)(2,1)S(1)}, bf16[2,1,1,1,16,6144]{5,4,3,2,1,0:T(8,128)(2,1)S(1)}, u32[]{:S(2)}, u32[]{:S(2)}) collective-permute-start(bf16[2,1,1,1,16,6144]{5,4,3,2,1,0:T(8,128)(2,1)S(1)} %pad_maximum_fusion.18), channel_id=1, source_target_pairs={{0,4},{1,5},{2,6},{3,7},{4,0},{5,1},{6,2},{7,3},{8,12},{9,13},{10,... | collective-permute-start | bytes 1179656 | tf_op jit(solution)/shard_map/ppermute | solution.py:46
  137.3 11.0 %collective-permute-start.21 = (bf16[2,1,1,1,16,6144]{5,4,3,2,1,0:T(8,128)(2,1)S(1)}, bf16[2,1,1,1,16,6144]{5,4,3,2,1,0:T(8,128)(2,1)S(1)}, u32[]{:S(2)}, u32[]{:S(2)}) collective-permute-start(bf16[2,1,1,1,16,6144]{5,4,3,2,1,0:T(8,128)(2,1)S(1)} %pad_maximum_fusion.19), channel_id=1, source_target_pairs={{0,2},{1,3},{2,0},{3,1},{4,6},{5,7},{6,4},{7,5},{8,10},{9,11},{10,... | collective-permute-start | bytes 1179656 | tf_op jit(solution)/shard_map/ppermute | solution.py:46
  145.7 19.5 %collective-permute-start.14 = (bf16[2,2,1,1,16,6144]{5,4,3,2,1,0:T(8,128)(2,1)S(1)}, bf16[2,2,1,1,16,6144]{5,4,3,2,1,0:T(8,128)(2,1)S(1)}, u32[]{:S(2)}, u32[]{:S(2)}) collective-permute-start(bf16[2,2,1,1,16,6144]{5,4,3,2,1,0:T(8,128)(2,1)S(1)} %pad_maximum_fusion.13), channel_id=1, source_target_pairs={{0,2},{1,3},{2,0},{3,1},{4,6},{5,7},{6,4},{7,5},{8,10},{9,11},{10,... | collective-permute-start | bytes 2359304 | tf_op jit(solution)/shard_map/ppermute | solution.py:46
  148.4 18.6 %collective-permute-start.22 = (bf16[2,1,2,1,16,6144]{5,4,3,2,1,0:T(8,128)(2,1)S(1)}, bf16[2,1,2,1,16,6144]{5,4,3,2,1,0:T(8,128)(2,1)S(1)}, u32[]{:S(2)}, u32[]{:S(2)}) collective-permute-start(bf16[2,1,2,1,16,6144]{5,4,3,2,1,0:T(8,128)(2,1)S(1)} %pad_maximum_fusion.14), channel_id=1, source_target_pairs={{0,4},{1,5},{2,6},{3,7},{4,0},{5,1},{6,2},{7,3},{8,12},{9,13},{10,... | collective-permute-start | bytes 2359304 | tf_op jit(solution)/shard_map/ppermute | solution.py:46
  165.4 3.5 %collective-permute-start.15 = (bf16[2,2,2,1,16,6144]{5,4,3,2,1,0:T(8,128)(2,1)S(1)}, bf16[2,2,2,1,16,6144]{5,4,3,2,1,0:T(8,128)(2,1)S(1)}, u32[]{:S(2)}, u32[]{:S(2)}) collective-permute-start(bf16[2,2,2,1,16,6144]{5,4,3,2,1,0:T(8,128)(2,1)S(1)} %pad_maximum_fusion.6), channel_id=1, source_target_pairs={{0,1},{1,0},{2,3},{3,2},{4,5},{5,4},{6,7},{7,6},{8,9},{9,8},{10,11... | collective-permute-start | bytes 4718600 | tf_op jit(solution)/shard_map/ppermute | solution.py:46
  167.1 4.0 %collective-permute-start.23 = (bf16[2,2,2,1,16,6144]{5,4,3,2,1,0:T(8,128)(2,1)S(1)}, bf16[2,2,2,1,16,6144]{5,4,3,2,1,0:T(8,128)(2,1)S(1)}, u32[]{:S(2)}, u32[]{:S(2)}) collective-permute-start(bf16[2,2,2,1,16,6144]{5,4,3,2,1,0:T(8,128)(2,1)S(1)} %pad_maximum_fusion.7), channel_id=1, source_target_pairs={{0,1},{1,0},{2,3},{3,2},{4,5},{5,4},{6,7},{7,6},{8,9},{9,8},{10,11... | collective-permute-start | bytes 4718600 | tf_op jit(solution)/shard_map/ppermute | solution.py:46
  178.2 21.8 %slice-start.6 = ((s8[6291456]{0:T(1024)(128)(4,1)}), s8[4194304]{0:T(1024)(128)(4,1)S(1)}, s32[]{:S(2)}) async-start(s8[6291456]{0:T(1024)(128)(4,1)} %bitcast.52), calls=%async_computation.6 | async-start | bytes 8388608
  185.6 14.4 %slice-start.7 = ((s8[6291456]{0:T(1024)(128)(4,1)}), s8[2097152]{0:T(1024)(128)(4,1)S(1)}, s32[]{:S(2)}) async-start(s8[6291456]{0:T(1024)(128)(4,1)} %bitcast.52), calls=%async_computation.7 | async-start | bytes 4194304
  209.1 1.3 collective-permute-start.24
  211.0 3.7 %collective-permute-start.25 = (f32[1]{0:T(128)}, f32[1]{0:T(128)}, u32[]{:S(2)}, u32[]{:S(2)}) collective-permute-start(f32[1]{0:T(128)} %add.89), channel_id=1, source_target_pairs={{0,2},{1,3},{2,0},{3,1},{4,6},{5,7},{6,4},{7,5},{8,10},{9,11},{10,... | collective-permute-start | bytes 20 | tf_op jit(solution)/shard_map/ppermute | solution.py:46
  215.3 3.7 %collective-permute-start.26 = (f32[1]{0:T(128)}, f32[1]{0:T(128)}, u32[]{:S(2)}, u32[]{:S(2)}) collective-permute-start(f32[1]{0:T(128)} %add.90), channel_id=1, source_target_pairs={{0,4},{1,5},{2,6},{3,7},{4,0},{5,1},{6,2},{7,3},{8,12},{9,13},{10,... | collective-permute-start | bytes 20 | tf_op jit(solution)/shard_map/ppermute | solution.py:46
  219.6 4.6 %collective-permute-start.27 = (f32[1]{0:T(128)}, f32[1]{0:T(128)}, u32[]{:S(2)}, u32[]{:S(2)}) collective-permute-start(f32[1]{0:T(128)} %add.91), channel_id=1, source_target_pairs={{0,8},{1,9},{2,10},{3,11},{4,12},{5,13},{6,14},{7,15},{8,0},{9,1},... | collective-permute-start | bytes 20 | tf_op jit(solution)/shard_map/ppermute | solution.py:46
  (15 other events, 95.2 us)

commit v2 on v1

--- a/solution.py
+++ b/solution.py
@@ -73,10 +73,19 @@
     return kept + swap(sent, bit, size).astype(jnp.float32)
 
 
-def add_over(value, size):
+def add_over(value, size, beside):
+    results = []
     for bit in range(size.bit_length() - 1):
-        value = value + swap(value, bit, size)
-    return value
+        if bit < len(beside):
+            operand, product = beside[bit]
+            value, operand = lax.optimization_barrier((value, operand))
+            result = product(operand)
+            other, result = lax.optimization_barrier((swap(value, bit, size), result))
+            results.append(result)
+        else:
+            other = swap(value, bit, size)
+        value = value + other
+    return value, results + [product(operand) for operand, product in beside[len(results) :]]
 
 
 def on_device(
@@ -125,20 +134,27 @@
     residual_own = ((outputs - target.astype(jnp.float32)) / total_rows).astype(jnp.bfloat16)
     tangent_own = (doutputs / total_rows).astype(jnp.bfloat16)
     residual_all, tangent_all = spread(residual_own, bits), spread(tangent_own, bits)
-    for stage in reversed(range(bits)):
+    hidden = lax.optimization_barrier(jnp.concatenate([hidden_tan, hidden_act], axis=0))
+    joined = jnp.zeros((2,) * (bits + 1) + (own_rows, width), jnp.bfloat16)
+    for stage in reversed(range(1, bits)):
+        if stage == 1:
+            joined, residual_all, tangent_all = lax.optimization_barrier(
+                (joined, residual_all, tangent_all)
+            )
         residual_all = gather_stage(residual_all, orders[0][stage], bits, size)
         tangent_all = gather_stage(tangent_all, orders[1][stage], bits, size)
-    scaled = lax.optimization_barrier(
-        jnp.concatenate(
-            [residual_all.reshape(total_rows, width), tangent_all.reshape(total_rows, width)],
-            axis=0,
-        )
-    )
-    hidden = lax.optimization_barrier(jnp.concatenate([hidden_tan, hidden_act], axis=0))
+    blocks = [residual_all, tangent_all]
+    others = [swap(block, 0, size) for block in blocks]
+    for side, parts in enumerate((blocks, others)):
+        for index, part in enumerate(parts):
+            start = [index] + [0] * (bits - 1) + [side, 0, 0]
+            joined = lax.dynamic_update_slice(joined, part[None], start)
+    scaled = lax.optimization_barrier(joined.reshape(2 * total_rows, width))
 
     back = contract_last(scaled, down_weight)
+    back_probe = contract_last(scaled[:total_rows], probe_down)
+    back, back_probe = lax.optimization_barrier((back, back_probe))
     back_hidden, back_tangent = back[:total_rows], back[total_rows:]
-    back_probe = contract_last(scaled[:total_rows], probe_down)
     curvature = (
         second_slope * tangent * back_hidden + first_slope * (back_tangent + back_probe)
     ).astype(jnp.bfloat16)
@@ -146,14 +162,15 @@
         tangent * curvature.astype(jnp.float32)
         + hidden_tan.astype(jnp.float32) * (back_probe - back_tangent)
     ) + jnp.sum(doutputs * tangent_own.astype(jnp.float32))
-    quadratic_form = add_over(jnp.reshape(local_sum, (1,)), size)
-    hessian_f32_up = contract_first(normed, curvature)
-    hessian_f32_down = contract_first(hidden, scaled)
-    return (
-        hessian_f32_up.astype(jnp.bfloat16),
-        hessian_f32_down.astype(jnp.bfloat16),
-        quadratic_form,
+    quadratic_form, (hessian_down, hessian_up) = add_over(
+        jnp.reshape(local_sum, (1,)),
+        size,
+        [
+            (hidden, lambda left: contract_first(left, scaled).astype(jnp.bfloat16)),
+            (curvature, lambda right: contract_first(normed, right).astype(jnp.bfloat16)),
+        ],
     )
+    return hessian_up, hessian_down, quadratic_form
 
 
 def solution(mesh):

time: 226 us -> 224 us (level)
  other arithmetic: 28.5 us -> 18.5 us
  local copies, waits for them, and re-layouts: 5.82 us -> 14.3 us
  starting transfers between devices: 27.1 us -> 31.5 us
  waiting for transfers between devices: 107 us -> 103 us
    concatenate x1 -> x0, other arithmetic: 5.28 us -> none  [on_device(): jnp.concatenate([residual_all.reshape(total_rows, width), tangent_all.res...]
    dynamic_update_slice x0 -> x4, local copies, waits for them, and re-layouts: none -> 5.02 us  [on_device(): joined = lax.dynamic_update_slice(joined, part[None], start)]
    ppermute x28, starting transfers between devices: 27.1 us -> 31.5 us  [swap(): return lax.ppermute(value, 'wide', pairs)]
    ppermute x28, waiting for transfers between devices: 107 us -> 103 us  [swap(): return lax.ppermute(value, 'wide', pairs)]
    convert_element_type x2, other arithmetic: 11.5 us -> 7.78 us  [probe_signs(): return jnp.where(odd, -size, size).astype(jnp.bfloat16)]
    broadcast_in_dim x0 -> x1, local copies, waits for them, and re-layouts: none -> 3.47 us  [on_device(): joined = jnp.zeros((2,) * (bits + 1) + (own_rows, width), jnp.bfloat16)]
    dot_general x2, matrix products: 15.9 us -> 13 us  [contract_last(): lax.dot_general(left, right, (((1,), (1,)), ((), ())), preferred_element_...]
    dot_general x2, matrix products: 13.7 us -> 16.4 us  [contract_first(): lax.dot_general(left, right, (((0,), (0,)), ((), ())), preferred_element_...]
  transfers between devices with their start and end apart: 28 -> 28, of which waited for: 23 -> 23; matrix products, arithmetic and copies ran while one was open for 11% -> 12% of each run, Pallas kernels for 0% -> 0%
where the time goes in v2:
time: 224 us
  waiting for transfers between devices  103 us (46%)
  matrix products  50.9 us (23%)
  starting transfers between devices  31.5 us (14%)
  other arithmetic  18.5 us (8%)
  local copies, waits for them, and re-layouts  14.3 us (6%)
  between operations  5.99 us (3%)
    ppermute x28, waiting for transfers between devices, swap(): return lax.ppermute(value, 'wide', pairs)  103 us
    ppermute x28, starting transfers between devices, swap(): return lax.ppermute(value, 'wide', pairs)  31.5 us
    dot_general x2, matrix products, contract_first(): lax.dot_general(left, right, (((0,), (0,)), ((), ())), preferred_element_...  16.4 us
    dot_general x2, matrix products, contract_last(): lax.dot_general(left, right, (((1,), (1,)), ((), ())), preferred_element_...  13 us
    convert_element_type x2, other arithmetic, probe_signs(): return jnp.where(odd, -size, size).astype(jnp.bfloat16)  7.78 us
    dot_general x1, matrix products, on_device(): preact = jnp.dot(normed, up_weight, preferred_element_type=jnp.float32)  6.91 us
    dynamic_update_slice x4, local copies, waits for them, and re-layouts, on_device(): joined = lax.dynamic_update_slice(joined, part[None], start)  5.02 us
    dot_general x1, matrix products, on_device(): jnp.dot(hidden_act, down_weight, preferred_element_type=jnp.float32)  4.54 us
  transfers between devices with their start and end apart: 28, of which 23 were waited for; matrix products, arithmetic and copies ran while one was open for 12% of the time, Pallas kernels for 0%

profile of v2, /device:TPU:0, one launch (start us, length us, event | category | flops | bytes accessed | tf_op | source)
XLA Modules:
  0.0 223.9 jit_solution(8407409254361820392)
XLA Ops:
  4.0 4.1 %collective-permute-start = (bf16[1,1,1,1,16,3072]{5,4,3,2,1,0:T(8,128)(2,1)S(1)}, bf16[1,1,1,1,16,3072]{5,4,3,2,1,0:T(8,128)(2,1)S(1)}, u32[]{:S(2)}, u32[]{:S(2)}) collective-permute-start(bf16[1,1,1,1,16,3072]{5,4,3,2,1,0:T(8,128)(2,1)S(1)} %get-tuple-element.52), channel_id=1, source_target_pairs={{0,8},{1,9},{2,10},{3,11},{4,12},{5,13},{6,14},{7,15},{8,0},{9,1},... | collective-permute-start | bytes 294920 | tf_op jit(solution)/shard_map/ppermute | solution.py:46
  9.9 3.6 %select_convert_fusion.1 = bf16[768,6144]{1,0:T(8,128)(2,1)S(1)} fusion(s32[6144]{0:T(1024)S(1)} %bitcast.68, s32[768]{0:T(1024)S(1)} %get-tuple-element.46), kind=kLoop, calls=%fused_computation.2 | loop fusion | flops 28311552 | bytes 9464832 | tf_op jit(solution)/shard_map/convert_element_type | solution.py:23
  13.5 2.4 %collective-permute-done = bf16[1,1,1,1,16,3072]{5,4,3,2,1,0:T(8,128)(2,1)S(1)} collective-permute-done((bf16[1,1,1,1,16,3072]{5,4,3,2,1,0:T(8,128)(2,1)S(1)}, bf16[1,1,1,1,16,3072]{5,4,3,2,1,0:T(8,128)(2,1)S(1)}, u32[]{:S(2)}, u32[]{:S(2)}) %collective-permute-start) | collective-permute-done | bytes 98336 | tf_op jit(solution)/shard_map/ppermute | solution.py:46
  18.9 2.8 %collective-permute-done.1 = bf16[2,1,1,1,16,3072]{5,4,3,2,1,0:T(8,128)(2,1)S(1)} collective-permute-done((bf16[2,1,1,1,16,3072]{5,4,3,2,1,0:T(8,128)(2,1)S(1)}, bf16[2,1,1,1,16,3072]{5,4,3,2,1,0:T(8,128)(2,1)S(1)}, u32[]{:S(2)}, u32[]{:S(2)}) %collective-permute-start.1) | collective-permute-done | bytes 196640 | tf_op jit(solution)/shard_map/ppermute | solution.py:46
  26.5 4.2 %select_convert_fusion = bf16[6144,768]{1,0:T(8,128)(2,1)S(1)} fusion(s32[768]{0:T(1024)S(1)} %get-tuple-element.45, s32[6144]{0:T(1024)S(1)} %bitcast.67), kind=kLoop, calls=%fused_computation | loop fusion | flops 28311552 | bytes 9464832 | tf_op jit(solution)/shard_map/convert_element_type | solution.py:23
  30.6 2.6 %collective-permute-done.5 = bf16[2,1,2,1,16,3072]{5,4,3,2,1,0:T(8,128)(2,1)S(1)} collective-permute-done((bf16[2,1,2,1,16,3072]{5,4,3,2,1,0:T(8,128)(2,1)S(1)}, bf16[2,1,2,1,16,3072]{5,4,3,2,1,0:T(8,128)(2,1)S(1)}, u32[]{:S(2)}, u32[]{:S(2)}) %collective-permute-start.5) | collective-permute-done | bytes 393248 | tf_op jit(solution)/shard_map/ppermute | solution.py:46
  38.5 6.9 %fusion.2 = f32[256,768]{1,0:T(8,128)S(1)} fusion(bf16[6144,768]{1,0:T(8,128)(2,1)} %param.10, bf16[256,3072]{1,0:T(8,128)(2,1)S(1)} %bitcast.64, bf16[256,3072]{1,0:T(8,128)(2,1)S(1)} %bitcast.61), kind=kOutput, calls=%fused_computation.25 | convolution fusion | flops 2422210560 | bytes 13369344 | tf_op jit(solution)/shard_map/dot_general | solution.py:117
  45.4 3.6 %multiply_convert_fusion = (bf16[256,768]{1,0:T(8,128)(2,1)S(1)}, bf16[256,768]{1,0:T(8,128)(2,1)S(1)}, f32[256,768]{1,0:T(8,128)}) fusion(f32[256,768]{1,0:T(8,128)S(1)} %fusion.2, bf16[6144,768]{1,0:T(8,128)(2,1)S(1)} %select_convert_fusion, bf16[256,3072]{1,0:T(8,128)(2,1)S(1)} %bitcast.65, bf16[256,3072]{1,0:T(8,128)(2,1)S(1)} %bitcast.62), kind=kOutput, calls=%fused_computation.46 | convolution fusion | flops 2424569856 | bytes 14942208 | tf_op jit(solution)/shard_map/dot_general | solution.py:122
  49.0 4.5 %fusion.30 = f32[256,6144]{1,0:T(8,128)} fusion(bf16[256,768]{1,0:T(8,128)(2,1)S(1)} %get-tuple-element.50, bf16[768,6144]{1,0:T(8,128)(2,1)S(1)} %bitcast.58), kind=kOutput, calls=%fused_computation.91 | convolution fusion | flops 2415919104 | bytes 16121856 | tf_op jit(solution)/shard_map/dot_general | solution.py:120
  53.6 3.2 %slice.159 = bf16[2,2,2,1,16,6144]{5,4,3,2,1,0:T(8,128)(2,1)} slice(f32[2,2,2,2,16,6144]{5,4,3,2,1,0:T(8,128)} %bitcast.6), slice={[0:2], [0:2], [0:2], [1:2], [0:16], [0:6144]} | slice | bytes 3145728 | tf_op jit(solution)/shard_map/slice | solution.py:72
  56.9 2.6 %fusion.31 = f32[256,6144]{1,0:T(8,128)S(1)} fusion(bf16[256,768]{1,0:T(8,128)(2,1)S(1)} %get-tuple-element.49, bf16[768,6144]{1,0:T(8,128)(2,1)S(1)} %bitcast.58), kind=kOutput, calls=%fused_computation.92 | convolution fusion | flops 2415919104 | bytes 16121856 | tf_op jit(solution)/shard_map/dot_general | solution.py:124
  59.5 3.9 %convolution_add_fusion = f32[256,6144]{1,0:T(8,128)S(1)} fusion(f32[256,6144]{1,0:T(8,128)S(1)} %fusion.31, bf16[256,768]{1,0:T(8,128)(2,1)} %copy-done, bf16[768,6144]{1,0:T(8,128)(2,1)S(1)} %select_convert_fusion.1), kind=kOutput, calls=%fused_computation.6 | convolution fusion | flops 2417491968 | bytes 22413312 | tf_op jit(solution)/shard_map/dot_general | solution.py:126
  63.4 2.8 %slice_add_fusion = f32[2,2,2,1,16,6144]{5,4,3,2,1,0:T(8,128)S(1)} fusion(f32[2,2,2,2,16,6144]{5,4,3,2,1,0:T(8,128)} %bitcast.6, bf16[2,2,2,1,16,6144]{5,4,3,2,1,0:T(8,128)(2,1)} %collective-permute-done.8), kind=kLoop, calls=%fused_computation.12 | loop fusion | flops 1572864 | bytes 7864320 | tf_op jit(solution)/shard_map/add | solution.py:73
  71.0 16.7 %collective-permute-done.9 = bf16[2,2,1,1,16,6144]{5,4,3,2,1,0:T(8,128)(2,1)S(1)} collective-permute-done((bf16[2,2,1,1,16,6144]{5,4,3,2,1,0:T(8,128)(2,1)S(1)}, bf16[2,2,1,1,16,6144]{5,4,3,2,1,0:T(8,128)(2,1)S(1)}, u32[]{:S(2)}, u32[]{:S(2)}) %collective-permute-start.9) | collective-permute-done | bytes 786464 | tf_op jit(solution)/shard_map/ppermute | solution.py:46
  88.3 2.7 %collective-permute-done.15 = bf16[2,1,2,1,16,6144]{5,4,2,1,0,3:T(8,128)(2,1)S(1)} collective-permute-done((bf16[2,1,2,1,16,6144]{5,4,2,1,0,3:T(8,128)(2,1)S(1)}, bf16[2,1,2,1,16,6144]{5,4,2,1,0,3:T(8,128)(2,1)S(1)}, u32[]{:S(2)}, u32[]{:S(2)}) %collective-permute-start.15) | collective-permute-done | bytes 786464 | tf_op jit(solution)/shard_map/ppermute | solution.py:46
  92.5 6.3 %collective-permute-done.10 = bf16[2,1,1,1,16,6144]{5,4,3,2,1,0:T(8,128)(2,1)S(1)} collective-permute-done((bf16[2,1,1,1,16,6144]{5,4,3,2,1,0:T(8,128)(2,1)S(1)}, bf16[2,1,1,1,16,6144]{5,4,3,2,1,0:T(8,128)(2,1)S(1)}, u32[]{:S(2)}, u32[]{:S(2)}) %collective-permute-start.10) | collective-permute-done | bytes 393248 | tf_op jit(solution)/shard_map/ppermute | solution.py:46
  99.0 3.6 %collective-permute-start.11 = (bf16[1,1,1,1,16,6144]{5,4,3,2,1,0:T(8,128)(2,1)S(1)}, bf16[1,1,1,1,16,6144]{5,4,3,2,1,0:T(8,128)(2,1)S(1)}, u32[]{:S(2)}, u32[]{:S(2)}) collective-permute-start(bf16[1,1,1,1,16,6144]{5,4,3,2,1,0:T(8,128)(2,1)S(1)} %slice.165), channel_id=1, source_target_pairs={{0,8},{1,9},{2,10},{3,11},{4,12},{5,13},{6,14},{7,15},{8,0},{9,1},... | collective-permute-start | bytes 589832 | tf_op jit(solution)/shard_map/ppermute | solution.py:46
  102.7 2.3 %collective-permute-start.17 = (bf16[1,1,1,1,16,6144]{5,4,2,1,0,3:T(8,128)(2,1)S(1)}, bf16[1,1,1,1,16,6144]{5,4,2,1,0,3:T(8,128)(2,1)S(1)}, u32[]{:S(2)}, u32[]{:S(2)}) collective-permute-start(bf16[1,1,1,1,16,6144]{5,4,2,1,0,3:T(8,128)(2,1)S(1)} %slice.164), channel_id=1, source_target_pairs={{0,8},{1,9},{2,10},{3,11},{4,12},{5,13},{6,14},{7,15},{8,0},{9,1},... | collective-permute-start | bytes 589832 | tf_op jit(solution)/shard_map/ppermute | solution.py:46
  105.0 10.0 %collective-permute-done.11 = bf16[1,1,1,1,16,6144]{5,4,3,2,1,0:T(8,128)(2,1)S(1)} collective-permute-done((bf16[1,1,1,1,16,6144]{5,4,3,2,1,0:T(8,128)(2,1)S(1)}, bf16[1,1,1,1,16,6144]{5,4,3,2,1,0:T(8,128)(2,1)S(1)}, u32[]{:S(2)}, u32[]{:S(2)}) %collective-permute-start.11) | collective-permute-done | bytes 196640 | tf_op jit(solution)/shard_map/ppermute | solution.py:46
  115.1 8.2 %collective-permute-done.17 = bf16[1,1,1,1,16,6144]{5,4,2,1,0,3:T(8,128)(2,1)S(1)} collective-permute-done((bf16[1,1,1,1,16,6144]{5,4,2,1,0,3:T(8,128)(2,1)S(1)}, bf16[1,1,1,1,16,6144]{5,4,2,1,0,3:T(8,128)(2,1)S(1)}, u32[]{:S(2)}, u32[]{:S(2)}) %collective-permute-start.17) | collective-permute-done | bytes 196640 | tf_op jit(solution)/shard_map/ppermute | solution.py:46
  123.5 8.3 %collective-permute-done.12 = bf16[1,1,1,1,16,6144]{5,4,3,2,1,0:T(8,128)(2,1)S(1)} collective-permute-done((bf16[1,1,1,1,16,6144]{5,4,3,2,1,0:T(8,128)(2,1)S(1)}, bf16[1,1,1,1,16,6144]{5,4,3,2,1,0:T(8,128)(2,1)S(1)}, u32[]{:S(2)}, u32[]{:S(2)}) %collective-permute-start.12) | collective-permute-done | bytes 196640 | tf_op jit(solution)/shard_map/ppermute | solution.py:46
  132.8 3.1 %collective-permute-done.18 = bf16[1,1,1,1,16,6144]{5,4,2,1,0,3:T(8,128)(2,1)S(1)} collective-permute-done((bf16[1,1,1,1,16,6144]{5,4,2,1,0,3:T(8,128)(2,1)S(1)}, bf16[1,1,1,1,16,6144]{5,4,2,1,0,3:T(8,128)(2,1)S(1)}, u32[]{:S(2)}, u32[]{:S(2)}) %collective-permute-start.18) | collective-permute-done | bytes 196640 | tf_op jit(solution)/shard_map/ppermute | solution.py:46
  137.6 6.7 %collective-permute-done.13 = bf16[2,1,1,1,16,6144]{5,4,3,2,1,0:T(8,128)(2,1)S(1)} collective-permute-done((bf16[2,1,1,1,16,6144]{5,4,3,2,1,0:T(8,128)(2,1)S(1)}, bf16[2,1,1,1,16,6144]{5,4,3,2,1,0:T(8,128)(2,1)S(1)}, u32[]{:S(2)}, u32[]{:S(2)}) %collective-permute-start.13) | collective-permute-done | bytes 393248 | tf_op jit(solution)/shard_map/ppermute | solution.py:46
  148.9 16.8 %collective-permute-done.20 = bf16[2,2,1,1,16,6144]{5,4,3,2,1,0:T(8,128)(2,1)S(1)} collective-permute-done((bf16[2,2,1,1,16,6144]{5,4,3,2,1,0:T(8,128)(2,1)S(1)}, bf16[2,2,1,1,16,6144]{5,4,3,2,1,0:T(8,128)(2,1)S(1)}, u32[]{:S(2)}, u32[]{:S(2)}) %collective-permute-start.20) | collective-permute-done | bytes 786464 | tf_op jit(solution)/shard_map/ppermute | solution.py:46
  165.8 3.5 %broadcast_in_dim.38 = bf16[2,2,2,2,2,16,6144]{6,5,4,3,2,1,0:T(8,128)(2,1)} broadcast(bf16[]{:T(256)} %constant.13.clone.1), dimensions={} | broadcast | bytes 6291458 | tf_op jit(solution)/shard_map/broadcast_in_dim | solution.py:138
  175.4 5.4 %fusion = f32[256,768]{1,0:T(8,128)} fusion(bf16[768,6144]{1,0:T(8,128)(2,1)S(1)} %select_convert_fusion.1, bf16[512,6144]{1,0:T(8,128)(2,1)} %bitcast.17), kind=kOutput, calls=%fused_computation.9 | convolution fusion | flops 2415919104 | bytes 13369344 | tf_op jit(solution)/shard_map/dot_general | solution.py:33
  180.9 7.6 %fusion.32 = f32[512,768]{1,0:T(8,128)S(1)} fusion(bf16[512,6144]{1,0:T(8,128)(2,1)} %bitcast.17, bf16[768,6144]{1,0:T(8,128)(2,1)S(1)} %bitcast.58), kind=kOutput, calls=%fused_computation.93 | convolution fusion | flops 4831838208 | bytes 17301504 | tf_op jit(solution)/shard_map/dot_general | solution.py:33
  191.1 10.5 %convolution_convert_fusion.1 = bf16[768,6144]{1,0:T(8,128)(2,1)} fusion(bf16[512,768]{1,0:T(8,128)(2,1)S(1)} %copy-done.11, bf16[512,6144]{1,0:T(8,128)(2,1)} %bitcast.17), kind=kOutput, calls=%fused_computation.5 | convolution fusion | flops 4836556800 | bytes 16515072 | tf_op jit(solution)/shard_map/dot_general | solution.py:39
  203.5 5.9 %convolution_convert_fusion = bf16[6144,768]{1,0:T(8,128)(2,1)} fusion(bf16[256,768]{1,0:T(8,128)(2,1)S(1)} %get-tuple-element.41, bf16[256,3072]{1,0:T(8,128)(2,1)S(1)} %bitcast.66, bf16[256,3072]{1,0:T(8,128)(2,1)S(1)} %bitcast.63), kind=kOutput, calls=%fused_computation.4 | convolution fusion | flops 2426929152 | bytes 12976128 | tf_op jit(solution)/shard_map/dot_general | solution.py:39
  209.4 2.8 %collective-permute-start.25 = (f32[1]{0:T(128)}, f32[1]{0:T(128)}, u32[]{:S(2)}, u32[]{:S(2)}) collective-permute-start(f32[1]{0:T(128)} %add.89), channel_id=1, source_target_pairs={{0,2},{1,3},{2,0},{3,1},{4,6},{5,7},{6,4},{7,5},{8,10},{9,11},{10,... | collective-permute-start | bytes 20 | tf_op jit(solution)/shard_map/ppermute | solution.py:46
  214.9 2.2 collective-permute-done.26
  219.1 3.1 %collective-permute-done.27 = f32[1]{0:T(128)} collective-permute-done((f32[1]{0:T(128)}, f32[1]{0:T(128)}, u32[]{:S(2)}, u32[]{:S(2)}) %collective-permute-start.27) | collective-permute-done | bytes 36 | tf_op jit(solution)/shard_map/ppermute | solution.py:46
  (117 shorter events, 45.1 us)
Async XLA Ops:
  4.0 11.9 %collective-permute-start = (bf16[1,1,1,1,16,3072]{5,4,3,2,1,0:T(8,128)(2,1)S(1)}, bf16[1,1,1,1,16,3072]{5,4,3,2,1,0:T(8,128)(2,1)S(1)}, u32[]{:S(2)}, u32[]{:S(2)}) collective-permute-start(bf16[1,1,1,1,16,3072]{5,4,3,2,1,0:T(8,128)(2,1)S(1)} %get-tuple-element.52), channel_id=1, source_target_pairs={{0,8},{1,9},{2,10},{3,11},{4,12},{5,13},{6,14},{7,15},{8,0},{9,1},... | collective-permute-start | bytes 294920 | tf_op jit(solution)/shard_map/ppermute | solution.py:46
  8.1 9.2 %collective-permute-start.2 = (bf16[1,1,1,1,16,3072]{5,4,3,2,1,0:T(8,128)(2,1)S(1)}, bf16[1,1,1,1,16,3072]{5,4,3,2,1,0:T(8,128)(2,1)S(1)}, u32[]{:S(2)}, u32[]{:S(2)}) collective-permute-start(bf16[1,1,1,1,16,3072]{5,4,3,2,1,0:T(8,128)(2,1)S(1)} %get-tuple-element.51), channel_id=1, source_target_pairs={{0,8},{1,9},{2,10},{3,11},{4,12},{5,13},{6,14},{7,15},{8,0},{9,1},... | collective-permute-start | bytes 294920 | tf_op jit(solution)/shard_map/ppermute | solution.py:46
  15.9 5.7 %collective-permute-start.1 = (bf16[2,1,1,1,16,3072]{5,4,3,2,1,0:T(8,128)(2,1)S(1)}, bf16[2,1,1,1,16,3072]{5,4,3,2,1,0:T(8,128)(2,1)S(1)}, u32[]{:S(2)}, u32[]{:S(2)}) collective-permute-start(bf16[2,1,1,1,16,3072]{5,4,3,2,1,0:T(8,128)(2,1)S(1)} %pad_maximum_fusion.15), channel_id=1, source_target_pairs={{0,4},{1,5},{2,6},{3,7},{4,0},{5,1},{6,2},{7,3},{8,12},{9,13},{10,... | collective-permute-start | bytes 589832 | tf_op jit(solution)/shard_map/ppermute | solution.py:46
  17.3 6.1 %collective-permute-start.3 = (bf16[2,1,1,1,16,3072]{5,4,3,2,1,0:T(8,128)(2,1)S(1)}, bf16[2,1,1,1,16,3072]{5,4,3,2,1,0:T(8,128)(2,1)S(1)}, u32[]{:S(2)}, u32[]{:S(2)}) collective-permute-start(bf16[2,1,1,1,16,3072]{5,4,3,2,1,0:T(8,128)(2,1)S(1)} %pad_maximum_fusion.16), channel_id=1, source_target_pairs={{0,2},{1,3},{2,0},{3,1},{4,6},{5,7},{6,4},{7,5},{8,10},{9,11},{10,... | collective-permute-start | bytes 589832 | tf_op jit(solution)/shard_map/ppermute | solution.py:46
  23.4 9.8 %collective-permute-start.5 = (bf16[2,1,2,1,16,3072]{5,4,3,2,1,0:T(8,128)(2,1)S(1)}, bf16[2,1,2,1,16,3072]{5,4,3,2,1,0:T(8,128)(2,1)S(1)}, u32[]{:S(2)}, u32[]{:S(2)}) collective-permute-start(bf16[2,1,2,1,16,3072]{5,4,3,2,1,0:T(8,128)(2,1)S(1)} %pad_maximum_fusion.12), channel_id=1, source_target_pairs={{0,4},{1,5},{2,6},{3,7},{4,0},{5,1},{6,2},{7,3},{8,12},{9,13},{10,... | collective-permute-start | bytes 1179656 | tf_op jit(solution)/shard_map/ppermute | solution.py:46
  24.9 9.8 %collective-permute-start.4 = (bf16[2,2,1,1,16,3072]{5,4,3,2,1,0:T(8,128)(2,1)S(1)}, bf16[2,2,1,1,16,3072]{5,4,3,2,1,0:T(8,128)(2,1)S(1)}, u32[]{:S(2)}, u32[]{:S(2)}) collective-permute-start(bf16[2,2,1,1,16,3072]{5,4,3,2,1,0:T(8,128)(2,1)S(1)} %pad_maximum_fusion.11), channel_id=1, source_target_pairs={{0,2},{1,3},{2,0},{3,1},{4,6},{5,7},{6,4},{7,5},{8,10},{9,11},{10,... | collective-permute-start | bytes 1179656 | tf_op jit(solution)/shard_map/ppermute | solution.py:46
  34.8 2.4 %collective-permute-start.6 = (bf16[2,2,2,1,16,3072]{5,4,3,2,1,0:T(8,128)(2,1)S(1)}, bf16[2,2,2,1,16,3072]{5,4,3,2,1,0:T(8,128)(2,1)S(1)}, u32[]{:S(2)}, u32[]{:S(2)}) collective-permute-start(bf16[2,2,2,1,16,3072]{5,4,3,2,1,0:T(8,128)(2,1)S(1)} %pad_maximum_fusion.6), channel_id=1, source_target_pairs={{0,1},{1,0},{2,3},{3,2},{4,5},{5,4},{6,7},{7,6},{8,9},{9,8},{10,11... | collective-permute-start | bytes 2359304 | tf_op jit(solution)/shard_map/ppermute | solution.py:46
  34.9 3.4 %collective-permute-start.7 = (bf16[2,2,2,1,16,3072]{5,4,3,2,1,0:T(8,128)(2,1)S(1)}, bf16[2,2,2,1,16,3072]{5,4,3,2,1,0:T(8,128)(2,1)S(1)}, u32[]{:S(2)}, u32[]{:S(2)}) collective-permute-start(bf16[2,2,2,1,16,3072]{5,4,3,2,1,0:T(8,128)(2,1)S(1)} %pad_maximum_fusion.7), channel_id=1, source_target_pairs={{0,1},{1,0},{2,3},{3,2},{4,5},{5,4},{6,7},{7,6},{8,9},{9,8},{10,11... | collective-permute-start | bytes 2359304 | tf_op jit(solution)/shard_map/ppermute | solution.py:46
  56.8 6.6 %collective-permute-start.8 = (bf16[2,2,2,1,16,6144]{5,4,3,2,1,0:T(8,128)(2,1)}, bf16[2,2,2,1,16,6144]{5,4,3,2,1,0:T(8,128)(2,1)}, u32[]{:S(2)}, u32[]{:S(2)}) collective-permute-start(bf16[2,2,2,1,16,6144]{5,4,3,2,1,0:T(8,128)(2,1)} %slice.159), channel_id=1, source_target_pairs={{0,1},{1,0},{2,3},{3,2},{4,5},{5,4},{6,7},{7,6},{8,9},{9,8},{10,11... | collective-permute-start | bytes 4718600 | tf_op jit(solution)/shard_map/ppermute | solution.py:46
  66.6 3.5 %collective-permute-start.14 = (bf16[2,2,2,1,16,6144]{5,4,2,1,0,3:T(8,128)(2,1)S(1)}, bf16[2,2,2,1,16,6144]{5,4,2,1,0,3:T(8,128)(2,1)S(1)}, u32[]{:S(2)}, u32[]{:S(2)}) collective-permute-start(bf16[2,2,2,1,16,6144]{5,4,2,1,0,3:T(8,128)(2,1)S(1)} %copy.19), channel_id=1, source_target_pairs={{0,1},{1,0},{2,3},{3,2},{4,5},{5,4},{6,7},{7,6},{8,9},{9,8},{10,11... | collective-permute-start | bytes 4718600 | tf_op jit(solution)/shard_map/ppermute | solution.py:46
  68.0 19.6 %collective-permute-start.9 = (bf16[2,2,1,1,16,6144]{5,4,3,2,1,0:T(8,128)(2,1)S(1)}, bf16[2,2,1,1,16,6144]{5,4,3,2,1,0:T(8,128)(2,1)S(1)}, u32[]{:S(2)}, u32[]{:S(2)}) collective-permute-start(bf16[2,2,1,1,16,6144]{5,4,3,2,1,0:T(8,128)(2,1)S(1)} %slice.161), channel_id=1, source_target_pairs={{0,2},{1,3},{2,0},{3,1},{4,6},{5,7},{6,4},{7,5},{8,10},{9,11},{10,... | collective-permute-start | bytes 2359304 | tf_op jit(solution)/shard_map/ppermute | solution.py:46
  70.5 44.4 %copy-start.2 = (bf16[16,6144]{1,0:T(8,128)(2,1)S(1)}, bf16[16,6144]{1,0:T(8,128)(2,1)}, u32[]{:S(2)}) copy-start(bf16[16,6144]{1,0:T(8,128)(2,1)} %param.7) | copy-start | bytes 589828
  70.5 44.4 %copy-start.12 = (bf16[16,6144]{1,0:T(8,128)(2,1)S(1)}, bf16[16,6144]{1,0:T(8,128)(2,1)}, u32[]{:S(2)}) copy-start(bf16[16,6144]{1,0:T(8,128)(2,1)} %param.8) | copy-start | bytes 589828
  70.5 20.4 %collective-permute-start.15 = (bf16[2,1,2,1,16,6144]{5,4,2,1,0,3:T(8,128)(2,1)S(1)}, bf16[2,1,2,1,16,6144]{5,4,2,1,0,3:T(8,128)(2,1)S(1)}, u32[]{:S(2)}, u32[]{:S(2)}) collective-permute-start(bf16[2,1,2,1,16,6144]{5,4,2,1,0,3:T(8,128)(2,1)S(1)} %slice.160), channel_id=1, source_target_pairs={{0,4},{1,5},{2,6},{3,7},{4,0},{5,1},{6,2},{7,3},{8,12},{9,13},{10,... | collective-permute-start | bytes 2359304 | tf_op jit(solution)/shard_map/ppermute | solution.py:46
  87.9 11.0 %collective-permute-start.10 = (bf16[2,1,1,1,16,6144]{5,4,3,2,1,0:T(8,128)(2,1)S(1)}, bf16[2,1,1,1,16,6144]{5,4,3,2,1,0:T(8,128)(2,1)S(1)}, u32[]{:S(2)}, u32[]{:S(2)}) collective-permute-start(bf16[2,1,1,1,16,6144]{5,4,3,2,1,0:T(8,128)(2,1)S(1)} %slice.163), channel_id=1, source_target_pairs={{0,4},{1,5},{2,6},{3,7},{4,0},{5,1},{6,2},{7,3},{8,12},{9,13},{10,... | collective-permute-start | bytes 1179656 | tf_op jit(solution)/shard_map/ppermute | solution.py:46
  91.2 11.4 %collective-permute-start.16 = (bf16[2,1,1,1,16,6144]{5,4,2,1,0,3:T(8,128)(2,1)S(1)}, bf16[2,1,1,1,16,6144]{5,4,2,1,0,3:T(8,128)(2,1)S(1)}, u32[]{:S(2)}, u32[]{:S(2)}) collective-permute-start(bf16[2,1,1,1,16,6144]{5,4,2,1,0,3:T(8,128)(2,1)S(1)} %slice.162), channel_id=1, source_target_pairs={{0,2},{1,3},{2,0},{3,1},{4,6},{5,7},{6,4},{7,5},{8,10},{9,11},{10,... | collective-permute-start | bytes 1179656 | tf_op jit(solution)/shard_map/ppermute | solution.py:46
  99.0 16.0 %collective-permute-start.11 = (bf16[1,1,1,1,16,6144]{5,4,3,2,1,0:T(8,128)(2,1)S(1)}, bf16[1,1,1,1,16,6144]{5,4,3,2,1,0:T(8,128)(2,1)S(1)}, u32[]{:S(2)}, u32[]{:S(2)}) collective-permute-start(bf16[1,1,1,1,16,6144]{5,4,3,2,1,0:T(8,128)(2,1)S(1)} %slice.165), channel_id=1, source_target_pairs={{0,8},{1,9},{2,10},{3,11},{4,12},{5,13},{6,14},{7,15},{8,0},{9,1},... | collective-permute-start | bytes 589832 | tf_op jit(solution)/shard_map/ppermute | solution.py:46
  102.7 20.7 %collective-permute-start.17 = (bf16[1,1,1,1,16,6144]{5,4,2,1,0,3:T(8,128)(2,1)S(1)}, bf16[1,1,1,1,16,6144]{5,4,2,1,0,3:T(8,128)(2,1)S(1)}, u32[]{:S(2)}, u32[]{:S(2)}) collective-permute-start(bf16[1,1,1,1,16,6144]{5,4,2,1,0,3:T(8,128)(2,1)S(1)} %slice.164), channel_id=1, source_target_pairs={{0,8},{1,9},{2,10},{3,11},{4,12},{5,13},{6,14},{7,15},{8,0},{9,1},... | collective-permute-start | bytes 589832 | tf_op jit(solution)/shard_map/ppermute | solution.py:46
  115.0 16.7 %collective-permute-start.12 = (bf16[1,1,1,1,16,6144]{5,4,3,2,1,0:T(8,128)(2,1)S(1)}, bf16[1,1,1,1,16,6144]{5,4,3,2,1,0:T(8,128)(2,1)S(1)}, u32[]{:S(2)}, u32[]{:S(2)}) collective-permute-start(bf16[1,1,1,1,16,6144]{5,4,3,2,1,0:T(8,128)(2,1)S(1)} %fusion.24), channel_id=1, source_target_pairs={{0,8},{1,9},{2,10},{3,11},{4,12},{5,13},{6,14},{7,15},{8,0},{9,1},... | collective-permute-start | bytes 589832 | tf_op jit(solution)/shard_map/ppermute | solution.py:46
  123.4 12.6 %collective-permute-start.18 = (bf16[1,1,1,1,16,6144]{5,4,2,1,0,3:T(8,128)(2,1)S(1)}, bf16[1,1,1,1,16,6144]{5,4,2,1,0,3:T(8,128)(2,1)S(1)}, u32[]{:S(2)}, u32[]{:S(2)}) collective-permute-start(bf16[1,1,1,1,16,6144]{5,4,2,1,0,3:T(8,128)(2,1)S(1)} %multiply_convert_fusion.2), channel_id=1, source_target_pairs={{0,8},{1,9},{2,10},{3,11},{4,12},{5,13},{6,14},{7,15},{8,0},{9,1},... | collective-permute-start | bytes 589832 | tf_op jit(solution)/shard_map/ppermute | solution.py:46
  131.8 12.5 %collective-permute-start.13 = (bf16[2,1,1,1,16,6144]{5,4,3,2,1,0:T(8,128)(2,1)S(1)}, bf16[2,1,1,1,16,6144]{5,4,3,2,1,0:T(8,128)(2,1)S(1)}, u32[]{:S(2)}, u32[]{:S(2)}) collective-permute-start(bf16[2,1,1,1,16,6144]{5,4,3,2,1,0:T(8,128)(2,1)S(1)} %pad_maximum_fusion.13), channel_id=1, source_target_pairs={{0,4},{1,5},{2,6},{3,7},{4,0},{5,1},{6,2},{7,3},{8,12},{9,13},{10,... | collective-permute-start | bytes 1179656 | tf_op jit(solution)/shard_map/ppermute | solution.py:46
  136.0 11.0 %collective-permute-start.19 = (bf16[2,1,1,1,16,6144]{5,4,2,1,0,3:T(8,128)(2,1)S(1)}, bf16[2,1,1,1,16,6144]{5,4,2,1,0,3:T(8,128)(2,1)S(1)}, u32[]{:S(2)}, u32[]{:S(2)}) collective-permute-start(bf16[2,1,1,1,16,6144]{5,4,2,1,0,3:T(8,128)(2,1)S(1)} %pad_maximum_fusion.14), channel_id=1, source_target_pairs={{0,2},{1,3},{2,0},{3,1},{4,6},{5,7},{6,4},{7,5},{8,10},{9,11},{10,... | collective-permute-start | bytes 1179656 | tf_op jit(solution)/shard_map/ppermute | solution.py:46
  147.1 18.6 %collective-permute-start.20 = (bf16[2,2,1,1,16,6144]{5,4,3,2,1,0:T(8,128)(2,1)S(1)}, bf16[2,2,1,1,16,6144]{5,4,3,2,1,0:T(8,128)(2,1)S(1)}, u32[]{:S(2)}, u32[]{:S(2)}) collective-permute-start(bf16[2,2,1,1,16,6144]{5,4,3,2,1,0:T(8,128)(2,1)S(1)} %pad_maximum_fusion.8), channel_id=1, source_target_pairs={{0,2},{1,3},{2,0},{3,1},{4,6},{5,7},{6,4},{7,5},{8,10},{9,11},{10,... | collective-permute-start | bytes 2359304 | tf_op jit(solution)/shard_map/ppermute | solution.py:46
  148.7 21.8 %collective-permute-start.21 = (bf16[2,1,2,1,16,6144]{5,4,2,1,0,3:T(8,128)(2,1)S(1)}, bf16[2,1,2,1,16,6144]{5,4,2,1,0,3:T(8,128)(2,1)S(1)}, u32[]{:S(2)}, u32[]{:S(2)}) collective-permute-start(bf16[2,1,2,1,16,6144]{5,4,2,1,0,3:T(8,128)(2,1)S(1)} %pad_maximum_fusion.9), channel_id=1, source_target_pairs={{0,4},{1,5},{2,6},{3,7},{4,0},{5,1},{6,2},{7,3},{8,12},{9,13},{10,... | collective-permute-start | bytes 2359304 | tf_op jit(solution)/shard_map/ppermute | solution.py:46
  165.7 6.7 %collective-permute-start.22 = (bf16[2,2,2,1,16,6144]{5,4,3,2,1,0:T(8,128)(2,1)S(1)}, bf16[2,2,2,1,16,6144]{5,4,3,2,1,0:T(8,128)(2,1)S(1)}, u32[]{:S(2)}, u32[]{:S(2)}) collective-permute-start(bf16[2,2,2,1,16,6144]{5,4,3,2,1,0:T(8,128)(2,1)S(1)} %constant_dynamic-update-slice_fusion), channel_id=1, source_target_pairs={{0,1},{1,0},{2,3},{3,2},{4,5},{5,4},{6,7},{7,6},{8,9},{9,8},{10,11... | collective-permute-start | bytes 4718600 | tf_op jit(solution)/shard_map/ppermute | solution.py:46
  170.6 3.6 %collective-permute-start.23 = (bf16[2,2,2,1,16,6144]{5,4,2,1,0,3:T(8,128)(2,1)S(1)}, bf16[2,2,2,1,16,6144]{5,4,2,1,0,3:T(8,128)(2,1)S(1)}, u32[]{:S(2)}, u32[]{:S(2)}) collective-permute-start(bf16[2,2,2,1,16,6144]{5,4,2,1,0,3:T(8,128)(2,1)S(1)} %constant_dynamic-update-slice_fusion.2), channel_id=1, source_target_pairs={{0,1},{1,0},{2,3},{3,2},{4,5},{5,4},{6,7},{7,6},{8,9},{9,8},{10,11... | collective-permute-start | bytes 4718600 | tf_op jit(solution)/shard_map/ppermute | solution.py:46
  191.0 12.5 %copy-start.4 = (bf16[2,2,2,2,16,3072]{5,4,3,2,1,0:T(8,128)(2,1)S(1)}, bf16[2,2,2,2,16,3072]{5,4,3,2,1,0:T(8,128)(2,1)}, u32[]{:S(2)}) copy-start(bf16[2,2,2,2,16,3072]{5,4,3,2,1,0:T(8,128)(2,1)} %copy-done.3) | copy-start | bytes 4718596
  191.0 12.5 %copy-start.6 = (bf16[2,2,2,2,16,3072]{5,4,3,2,1,0:T(8,128)(2,1)S(1)}, bf16[2,2,2,2,16,3072]{5,4,3,2,1,0:T(8,128)(2,1)}, u32[]{:S(2)}) copy-start(bf16[2,2,2,2,16,3072]{5,4,3,2,1,0:T(8,128)(2,1)} %copy-done.5) | copy-start | bytes 4718596
  201.5 1.3 collective-permute-start.24
  209.4 3.5 %collective-permute-start.25 = (f32[1]{0:T(128)}, f32[1]{0:T(128)}, u32[]{:S(2)}, u32[]{:S(2)}) collective-permute-start(f32[1]{0:T(128)} %add.89), channel_id=1, source_target_pairs={{0,2},{1,3},{2,0},{3,1},{4,6},{5,7},{6,4},{7,5},{8,10},{9,11},{10,... | collective-permute-start | bytes 20 | tf_op jit(solution)/shard_map/ppermute | solution.py:46
  213.5 3.6 %collective-permute-start.26 = (f32[1]{0:T(128)}, f32[1]{0:T(128)}, u32[]{:S(2)}, u32[]{:S(2)}) collective-permute-start(f32[1]{0:T(128)} %add.90), channel_id=1, source_target_pairs={{0,4},{1,5},{2,6},{3,7},{4,0},{5,1},{6,2},{7,3},{8,12},{9,13},{10,... | collective-permute-start | bytes 20 | tf_op jit(solution)/shard_map/ppermute | solution.py:46
  217.7 4.5 %collective-permute-start.27 = (f32[1]{0:T(128)}, f32[1]{0:T(128)}, u32[]{:S(2)}, u32[]{:S(2)}) collective-permute-start(f32[1]{0:T(128)} %add.91), channel_id=1, source_target_pairs={{0,8},{1,9},{2,10},{3,11},{4,12},{5,13},{6,14},{7,15},{8,0},{9,1},... | collective-permute-start | bytes 20 | tf_op jit(solution)/shard_map/ppermute | solution.py:46
  (12 other events, 87.9 us)

commit v3 on v2

--- a/solution.py
+++ b/solution.py
@@ -135,7 +135,9 @@
     tangent_own = (doutputs / total_rows).astype(jnp.bfloat16)
     residual_all, tangent_all = spread(residual_own, bits), spread(tangent_own, bits)
     hidden = lax.optimization_barrier(jnp.concatenate([hidden_tan, hidden_act], axis=0))
-    joined = jnp.zeros((2,) * (bits + 1) + (own_rows, width), jnp.bfloat16)
+    joined = jnp.broadcast_to(
+        norm_gain[0].astype(jnp.bfloat16), (2,) * (bits + 1) + (own_rows, width)
+    )
     for stage in reversed(range(1, bits)):
         if stage == 1:
             joined, residual_all, tangent_all = lax.optimization_barrier(
@@ -162,12 +164,12 @@
         tangent * curvature.astype(jnp.float32)
         + hidden_tan.astype(jnp.float32) * (back_probe - back_tangent)
     ) + jnp.sum(doutputs * tangent_own.astype(jnp.float32))
-    quadratic_form, (hessian_down, hessian_up) = add_over(
+    quadratic_form, (hessian_up, hessian_down) = add_over(
         jnp.reshape(local_sum, (1,)),
         size,
         [
+            (curvature, lambda right: contract_first(normed, right).astype(jnp.bfloat16)),
             (hidden, lambda left: contract_first(left, scaled).astype(jnp.bfloat16)),
-            (curvature, lambda right: contract_first(normed, right).astype(jnp.bfloat16)),
         ],
     )
     return hessian_up, hessian_down, quadratic_form

time: 224 us -> 227 us (1.013)
  transfers between devices with their start and end apart: 28 -> 28, of which waited for: 23 -> 24; matrix products, arithmetic and copies ran while one was open for 12% -> 11% of each run, Pallas kernels for 0% -> 0%
where the time goes in v3:
time: 227 us
  waiting for transfers between devices  103 us (45%)
  matrix products  52.7 us (23%)
  starting transfers between devices  29.9 us (13%)
  other arithmetic  18.6 us (8%)
  local copies, waits for them, and re-layouts  16.2 us (7%)
  between operations  6.09 us (3%)
    ppermute x28, waiting for transfers between devices, swap(): return lax.ppermute(value, 'wide', pairs)  103 us
    ppermute x28, starting transfers between devices, swap(): return lax.ppermute(value, 'wide', pairs)  29.9 us
    dot_general x2, matrix products, contract_first(): lax.dot_general(left, right, (((0,), (0,)), ((), ())), preferred_element_...  18.2 us
    dot_general x2, matrix products, contract_last(): lax.dot_general(left, right, (((1,), (1,)), ((), ())), preferred_element_...  13 us
    convert_element_type x2, other arithmetic, probe_signs(): return jnp.where(odd, -size, size).astype(jnp.bfloat16)  7.78 us
    dot_general x1, matrix products, on_device(): preact = jnp.dot(normed, up_weight, preferred_element_type=jnp.float32)  6.91 us
    dynamic_update_slice x4, local copies, waits for them, and re-layouts, on_device(): joined = lax.dynamic_update_slice(joined, part[None], start)  5.12 us
  transfers between devices with their start and end apart: 28, of which 24 were waited for; matrix products, arithmetic and copies ran while one was open for 11% of the time, Pallas kernels for 0%

profile of v3, /device:TPU:0, one launch (start us, length us, event | category | flops | bytes accessed | tf_op | source)
XLA Modules:
  0.0 226.8 jit_solution(17461403471591806040)
XLA Ops:
  4.0 4.1 %collective-permute-start = (bf16[1,1,1,1,16,3072]{5,4,3,2,1,0:T(8,128)(2,1)S(1)}, bf16[1,1,1,1,16,3072]{5,4,3,2,1,0:T(8,128)(2,1)S(1)}, u32[]{:S(2)}, u32[]{:S(2)}) collective-permute-start(bf16[1,1,1,1,16,3072]{5,4,3,2,1,0:T(8,128)(2,1)S(1)} %get-tuple-element.52), channel_id=1, source_target_pairs={{0,8},{1,9},{2,10},{3,11},{4,12},{5,13},{6,14},{7,15},{8,0},{9,1},... | collective-permute-start | bytes 294920 | tf_op jit(solution)/shard_map/ppermute | solution.py:46
  9.9 3.6 %select_convert_fusion.1 = bf16[768,6144]{1,0:T(8,128)(2,1)S(1)} fusion(s32[6144]{0:T(1024)S(1)} %bitcast.69, s32[768]{0:T(1024)S(1)} %get-tuple-element.46), kind=kLoop, calls=%fused_computation.2 | loop fusion | flops 28311552 | bytes 9464832 | tf_op jit(solution)/shard_map/convert_element_type | solution.py:23
  13.5 2.4 %collective-permute-done = bf16[1,1,1,1,16,3072]{5,4,3,2,1,0:T(8,128)(2,1)S(1)} collective-permute-done((bf16[1,1,1,1,16,3072]{5,4,3,2,1,0:T(8,128)(2,1)S(1)}, bf16[1,1,1,1,16,3072]{5,4,3,2,1,0:T(8,128)(2,1)S(1)}, u32[]{:S(2)}, u32[]{:S(2)}) %collective-permute-start) | collective-permute-done | bytes 98336 | tf_op jit(solution)/shard_map/ppermute | solution.py:46
  18.9 2.8 %collective-permute-done.1 = bf16[2,1,1,1,16,3072]{5,4,3,2,1,0:T(8,128)(2,1)S(1)} collective-permute-done((bf16[2,1,1,1,16,3072]{5,4,3,2,1,0:T(8,128)(2,1)S(1)}, bf16[2,1,1,1,16,3072]{5,4,3,2,1,0:T(8,128)(2,1)S(1)}, u32[]{:S(2)}, u32[]{:S(2)}) %collective-permute-start.1) | collective-permute-done | bytes 196640 | tf_op jit(solution)/shard_map/ppermute | solution.py:46
  26.5 4.2 %select_convert_fusion = bf16[6144,768]{1,0:T(8,128)(2,1)S(1)} fusion(s32[768]{0:T(1024)S(1)} %get-tuple-element.45, s32[6144]{0:T(1024)S(1)} %bitcast.68), kind=kLoop, calls=%fused_computation | loop fusion | flops 28311552 | bytes 9464832 | tf_op jit(solution)/shard_map/convert_element_type | solution.py:23
  30.6 2.6 %collective-permute-done.5 = bf16[2,1,2,1,16,3072]{5,4,3,2,1,0:T(8,128)(2,1)S(1)} collective-permute-done((bf16[2,1,2,1,16,3072]{5,4,3,2,1,0:T(8,128)(2,1)S(1)}, bf16[2,1,2,1,16,3072]{5,4,3,2,1,0:T(8,128)(2,1)S(1)}, u32[]{:S(2)}, u32[]{:S(2)}) %collective-permute-start.5) | collective-permute-done | bytes 393248 | tf_op jit(solution)/shard_map/ppermute | solution.py:46
  35.4 1.8 collective-permute-done.6
  38.5 6.9 %fusion.2 = f32[256,768]{1,0:T(8,128)S(1)} fusion(bf16[6144,768]{1,0:T(8,128)(2,1)} %param.10, bf16[256,3072]{1,0:T(8,128)(2,1)S(1)} %bitcast.65, bf16[256,3072]{1,0:T(8,128)(2,1)S(1)} %bitcast.62), kind=kOutput, calls=%fused_computation.25 | convolution fusion | flops 2422210560 | bytes 13369344 | tf_op jit(solution)/shard_map/dot_general | solution.py:117
  45.4 3.6 %multiply_convert_fusion = (bf16[256,768]{1,0:T(8,128)(2,1)S(1)}, bf16[256,768]{1,0:T(8,128)(2,1)S(1)}, f32[256,768]{1,0:T(8,128)}) fusion(f32[256,768]{1,0:T(8,128)S(1)} %fusion.2, bf16[6144,768]{1,0:T(8,128)(2,1)S(1)} %select_convert_fusion, bf16[256,3072]{1,0:T(8,128)(2,1)S(1)} %bitcast.66, bf16[256,3072]{1,0:T(8,128)(2,1)S(1)} %bitcast.63), kind=kOutput, calls=%fused_computation.46 | convolution fusion | flops 2424569856 | bytes 14942208 | tf_op jit(solution)/shard_map/dot_general | solution.py:122
  49.0 4.5 %fusion.30 = f32[256,6144]{1,0:T(8,128)} fusion(bf16[256,768]{1,0:T(8,128)(2,1)S(1)} %get-tuple-element.50, bf16[768,6144]{1,0:T(8,128)(2,1)S(1)} %bitcast.59), kind=kOutput, calls=%fused_computation.91 | convolution fusion | flops 2415919104 | bytes 16121856 | tf_op jit(solution)/shard_map/dot_general | solution.py:120
  53.5 3.2 %slice.165 = bf16[2,2,2,1,16,6144]{5,4,3,2,1,0:T(8,128)(2,1)} slice(f32[2,2,2,2,16,6144]{5,4,3,2,1,0:T(8,128)} %bitcast.7), slice={[0:2], [0:2], [0:2], [1:2], [0:16], [0:6144]} | slice | bytes 3145728 | tf_op jit(solution)/shard_map/slice | solution.py:72
  56.9 2.6 %fusion.31 = f32[256,6144]{1,0:T(8,128)S(1)} fusion(bf16[256,768]{1,0:T(8,128)(2,1)S(1)} %get-tuple-element.49, bf16[768,6144]{1,0:T(8,128)(2,1)S(1)} %bitcast.59), kind=kOutput, calls=%fused_computation.92 | convolution fusion | flops 2415919104 | bytes 16121856 | tf_op jit(solution)/shard_map/dot_general | solution.py:124
  59.5 3.9 %convolution_add_fusion = f32[256,6144]{1,0:T(8,128)S(1)} fusion(f32[256,6144]{1,0:T(8,128)S(1)} %fusion.31, bf16[256,768]{1,0:T(8,128)(2,1)} %copy-done, bf16[768,6144]{1,0:T(8,128)(2,1)S(1)} %select_convert_fusion.1), kind=kOutput, calls=%fused_computation.6 | convolution fusion | flops 2417491968 | bytes 22413312 | tf_op jit(solution)/shard_map/dot_general | solution.py:126
  63.4 2.8 %slice_add_fusion = f32[2,2,2,1,16,6144]{5,4,3,2,1,0:T(8,128)S(1)} fusion(f32[2,2,2,2,16,6144]{5,4,3,2,1,0:T(8,128)} %bitcast.7, bf16[2,2,2,1,16,6144]{5,4,3,2,1,0:T(8,128)(2,1)} %collective-permute-done.8), kind=kLoop, calls=%fused_computation.12 | loop fusion | flops 1572864 | bytes 7864320 | tf_op jit(solution)/shard_map/add | solution.py:73
  71.5 17.4 %collective-permute-done.9 = bf16[2,2,1,1,16,6144]{5,4,3,2,1,0:T(8,128)(2,1)S(1)} collective-permute-done((bf16[2,2,1,1,16,6144]{5,4,3,2,1,0:T(8,128)(2,1)S(1)}, bf16[2,2,1,1,16,6144]{5,4,3,2,1,0:T(8,128)(2,1)S(1)}, u32[]{:S(2)}, u32[]{:S(2)}) %collective-permute-start.9) | collective-permute-done | bytes 786464 | tf_op jit(solution)/shard_map/ppermute | solution.py:46
  91.9 7.5 %collective-permute-done.10 = bf16[2,1,1,1,16,6144]{5,4,3,2,1,0:T(8,128)(2,1)S(1)} collective-permute-done((bf16[2,1,1,1,16,6144]{5,4,3,2,1,0:T(8,128)(2,1)S(1)}, bf16[2,1,1,1,16,6144]{5,4,3,2,1,0:T(8,128)(2,1)S(1)}, u32[]{:S(2)}, u32[]{:S(2)}) %collective-permute-start.10) | collective-permute-done | bytes 393248 | tf_op jit(solution)/shard_map/ppermute | solution.py:46
  99.5 3.7 %collective-permute-start.11 = (bf16[1,1,1,1,16,6144]{5,4,3,2,1,0:T(8,128)(2,1)S(1)}, bf16[1,1,1,1,16,6144]{5,4,3,2,1,0:T(8,128)(2,1)S(1)}, u32[]{:S(2)}, u32[]{:S(2)}) collective-permute-start(bf16[1,1,1,1,16,6144]{5,4,3,2,1,0:T(8,128)(2,1)S(1)} %slice.171), channel_id=1, source_target_pairs={{0,8},{1,9},{2,10},{3,11},{4,12},{5,13},{6,14},{7,15},{8,0},{9,1},... | collective-permute-start | bytes 589832 | tf_op jit(solution)/shard_map/ppermute | solution.py:46
  104.7 10.4 %collective-permute-done.11 = bf16[1,1,1,1,16,6144]{5,4,3,2,1,0:T(8,128)(2,1)S(1)} collective-permute-done((bf16[1,1,1,1,16,6144]{5,4,3,2,1,0:T(8,128)(2,1)S(1)}, bf16[1,1,1,1,16,6144]{5,4,3,2,1,0:T(8,128)(2,1)S(1)}, u32[]{:S(2)}, u32[]{:S(2)}) %collective-permute-start.11) | collective-permute-done | bytes 196640 | tf_op jit(solution)/shard_map/ppermute | solution.py:46
  115.3 8.2 %collective-permute-done.17 = bf16[1,1,1,1,16,6144]{5,4,2,1,0,3:T(8,128)(2,1)S(1)} collective-permute-done((bf16[1,1,1,1,16,6144]{5,4,2,1,0,3:T(8,128)(2,1)S(1)}, bf16[1,1,1,1,16,6144]{5,4,2,1,0,3:T(8,128)(2,1)S(1)}, u32[]{:S(2)}, u32[]{:S(2)}) %collective-permute-start.17) | collective-permute-done | bytes 196640 | tf_op jit(solution)/shard_map/ppermute | solution.py:46
  123.7 8.3 %collective-permute-done.12 = bf16[1,1,1,1,16,6144]{5,4,3,2,1,0:T(8,128)(2,1)S(1)} collective-permute-done((bf16[1,1,1,1,16,6144]{5,4,3,2,1,0:T(8,128)(2,1)S(1)}, bf16[1,1,1,1,16,6144]{5,4,3,2,1,0:T(8,128)(2,1)S(1)}, u32[]{:S(2)}, u32[]{:S(2)}) %collective-permute-start.12) | collective-permute-done | bytes 196640 | tf_op jit(solution)/shard_map/ppermute | solution.py:46
  132.8 3.3 %collective-permute-done.18 = bf16[1,1,1,1,16,6144]{5,4,2,1,0,3:T(8,128)(2,1)S(1)} collective-permute-done((bf16[1,1,1,1,16,6144]{5,4,2,1,0,3:T(8,128)(2,1)S(1)}, bf16[1,1,1,1,16,6144]{5,4,2,1,0,3:T(8,128)(2,1)S(1)}, u32[]{:S(2)}, u32[]{:S(2)}) %collective-permute-start.18) | collective-permute-done | bytes 196640 | tf_op jit(solution)/shard_map/ppermute | solution.py:46
  137.7 6.7 %collective-permute-done.13 = bf16[2,1,1,1,16,6144]{5,4,3,2,1,0:T(8,128)(2,1)S(1)} collective-permute-done((bf16[2,1,1,1,16,6144]{5,4,3,2,1,0:T(8,128)(2,1)S(1)}, bf16[2,1,1,1,16,6144]{5,4,3,2,1,0:T(8,128)(2,1)S(1)}, u32[]{:S(2)}, u32[]{:S(2)}) %collective-permute-start.13) | collective-permute-done | bytes 393248 | tf_op jit(solution)/shard_map/ppermute | solution.py:46
  145.2 1.8 collective-permute-done.19
  147.1 4.0 %broadcast_in_dim.38 = bf16[2,2,2,2,2,16,6144]{6,5,4,3,2,1,0:T(8,128)(2,1)} broadcast(bf16[]{:T(256)} %bitcast.6), dimensions={} | broadcast | bytes 6291458 | tf_op jit(solution)/shard_map/broadcast_in_dim | solution.py:138
  152.9 16.7 %collective-permute-done.20 = bf16[2,2,1,1,16,6144]{5,4,3,2,1,0:T(8,128)(2,1)S(1)} collective-permute-done((bf16[2,2,1,1,16,6144]{5,4,3,2,1,0:T(8,128)(2,1)S(1)}, bf16[2,2,1,1,16,6144]{5,4,3,2,1,0:T(8,128)(2,1)S(1)}, u32[]{:S(2)}, u32[]{:S(2)}) %collective-permute-start.20) | collective-permute-done | bytes 786464 | tf_op jit(solution)/shard_map/ppermute | solution.py:46
  176.6 5.4 %fusion = f32[256,768]{1,0:T(8,128)} fusion(bf16[768,6144]{1,0:T(8,128)(2,1)S(1)} %select_convert_fusion.1, bf16[512,6144]{1,0:T(8,128)(2,1)} %bitcast.18), kind=kOutput, calls=%fused_computation.9 | convolution fusion | flops 2415919104 | bytes 13369344 | tf_op jit(solution)/shard_map/dot_general | solution.py:33
  182.1 7.6 %fusion.32 = f32[512,768]{1,0:T(8,128)S(1)} fusion(bf16[512,6144]{1,0:T(8,128)(2,1)} %bitcast.18, bf16[768,6144]{1,0:T(8,128)(2,1)S(1)} %bitcast.59), kind=kOutput, calls=%fused_computation.93 | convolution fusion | flops 4831838208 | bytes 17301504 | tf_op jit(solution)/shard_map/dot_general | solution.py:33
  192.3 7.9 %convolution_convert_fusion = bf16[6144,768]{1,0:T(8,128)(2,1)} fusion(bf16[256,768]{1,0:T(8,128)(2,1)S(1)} %get-tuple-element.38, bf16[256,3072]{1,0:T(8,128)(2,1)} %bitcast.67, bf16[256,3072]{1,0:T(8,128)(2,1)S(1)} %bitcast.64), kind=kOutput, calls=%fused_computation.4 | convolution fusion | flops 2426929152 | bytes 12976128 | tf_op jit(solution)/shard_map/dot_general | solution.py:39
  202.0 10.3 %convolution_convert_fusion.1 = bf16[768,6144]{1,0:T(8,128)(2,1)} fusion(bf16[512,768]{1,0:T(8,128)(2,1)S(1)} %copy-done.10, bf16[512,6144]{1,0:T(8,128)(2,1)} %bitcast.18), kind=kOutput, calls=%fused_computation.5 | convolution fusion | flops 4836556800 | bytes 16515072 | tf_op jit(solution)/shard_map/dot_general | solution.py:39
  212.3 2.8 %collective-permute-start.25 = (f32[1]{0:T(128)}, f32[1]{0:T(128)}, u32[]{:S(2)}, u32[]{:S(2)}) collective-permute-start(f32[1]{0:T(128)} %add.89), channel_id=1, source_target_pairs={{0,2},{1,3},{2,0},{3,1},{4,6},{5,7},{6,4},{7,5},{8,10},{9,11},{10,... | collective-permute-start | bytes 20 | tf_op jit(solution)/shard_map/ppermute | solution.py:46
  217.8 2.2 collective-permute-done.26
  222.0 3.1 %collective-permute-done.27 = f32[1]{0:T(128)} collective-permute-done((f32[1]{0:T(128)}, f32[1]{0:T(128)}, u32[]{:S(2)}, u32[]{:S(2)}) %collective-permute-start.27) | collective-permute-done | bytes 36 | tf_op jit(solution)/shard_map/ppermute | solution.py:46
  (116 shorter events, 44.4 us)
Async XLA Ops:
  4.0 11.9 %collective-permute-start = (bf16[1,1,1,1,16,3072]{5,4,3,2,1,0:T(8,128)(2,1)S(1)}, bf16[1,1,1,1,16,3072]{5,4,3,2,1,0:T(8,128)(2,1)S(1)}, u32[]{:S(2)}, u32[]{:S(2)}) collective-permute-start(bf16[1,1,1,1,16,3072]{5,4,3,2,1,0:T(8,128)(2,1)S(1)} %get-tuple-element.52), channel_id=1, source_target_pairs={{0,8},{1,9},{2,10},{3,11},{4,12},{5,13},{6,14},{7,15},{8,0},{9,1},... | collective-permute-start | bytes 294920 | tf_op jit(solution)/shard_map/ppermute | solution.py:46
  8.1 9.2 %collective-permute-start.2 = (bf16[1,1,1,1,16,3072]{5,4,3,2,1,0:T(8,128)(2,1)S(1)}, bf16[1,1,1,1,16,3072]{5,4,3,2,1,0:T(8,128)(2,1)S(1)}, u32[]{:S(2)}, u32[]{:S(2)}) collective-permute-start(bf16[1,1,1,1,16,3072]{5,4,3,2,1,0:T(8,128)(2,1)S(1)} %get-tuple-element.51), channel_id=1, source_target_pairs={{0,8},{1,9},{2,10},{3,11},{4,12},{5,13},{6,14},{7,15},{8,0},{9,1},... | collective-permute-start | bytes 294920 | tf_op jit(solution)/shard_map/ppermute | solution.py:46
  15.9 5.7 %collective-permute-start.1 = (bf16[2,1,1,1,16,3072]{5,4,3,2,1,0:T(8,128)(2,1)S(1)}, bf16[2,1,1,1,16,3072]{5,4,3,2,1,0:T(8,128)(2,1)S(1)}, u32[]{:S(2)}, u32[]{:S(2)}) collective-permute-start(bf16[2,1,1,1,16,3072]{5,4,3,2,1,0:T(8,128)(2,1)S(1)} %pad_maximum_fusion.15), channel_id=1, source_target_pairs={{0,4},{1,5},{2,6},{3,7},{4,0},{5,1},{6,2},{7,3},{8,12},{9,13},{10,... | collective-permute-start | bytes 589832 | tf_op jit(solution)/shard_map/ppermute | solution.py:46
  17.3 6.1 %collective-permute-start.3 = (bf16[2,1,1,1,16,3072]{5,4,3,2,1,0:T(8,128)(2,1)S(1)}, bf16[2,1,1,1,16,3072]{5,4,3,2,1,0:T(8,128)(2,1)S(1)}, u32[]{:S(2)}, u32[]{:S(2)}) collective-permute-start(bf16[2,1,1,1,16,3072]{5,4,3,2,1,0:T(8,128)(2,1)S(1)} %pad_maximum_fusion.16), channel_id=1, source_target_pairs={{0,2},{1,3},{2,0},{3,1},{4,6},{5,7},{6,4},{7,5},{8,10},{9,11},{10,... | collective-permute-start | bytes 589832 | tf_op jit(solution)/shard_map/ppermute | solution.py:46
  23.4 9.8 %collective-permute-start.5 = (bf16[2,1,2,1,16,3072]{5,4,3,2,1,0:T(8,128)(2,1)S(1)}, bf16[2,1,2,1,16,3072]{5,4,3,2,1,0:T(8,128)(2,1)S(1)}, u32[]{:S(2)}, u32[]{:S(2)}) collective-permute-start(bf16[2,1,2,1,16,3072]{5,4,3,2,1,0:T(8,128)(2,1)S(1)} %pad_maximum_fusion.12), channel_id=1, source_target_pairs={{0,4},{1,5},{2,6},{3,7},{4,0},{5,1},{6,2},{7,3},{8,12},{9,13},{10,... | collective-permute-start | bytes 1179656 | tf_op jit(solution)/shard_map/ppermute | solution.py:46
  24.9 9.8 %collective-permute-start.4 = (bf16[2,2,1,1,16,3072]{5,4,3,2,1,0:T(8,128)(2,1)S(1)}, bf16[2,2,1,1,16,3072]{5,4,3,2,1,0:T(8,128)(2,1)S(1)}, u32[]{:S(2)}, u32[]{:S(2)}) collective-permute-start(bf16[2,2,1,1,16,3072]{5,4,3,2,1,0:T(8,128)(2,1)S(1)} %pad_maximum_fusion.11), channel_id=1, source_target_pairs={{0,2},{1,3},{2,0},{3,1},{4,6},{5,7},{6,4},{7,5},{8,10},{9,11},{10,... | collective-permute-start | bytes 1179656 | tf_op jit(solution)/shard_map/ppermute | solution.py:46
  34.8 2.4 %collective-permute-start.6 = (bf16[2,2,2,1,16,3072]{5,4,3,2,1,0:T(8,128)(2,1)S(1)}, bf16[2,2,2,1,16,3072]{5,4,3,2,1,0:T(8,128)(2,1)S(1)}, u32[]{:S(2)}, u32[]{:S(2)}) collective-permute-start(bf16[2,2,2,1,16,3072]{5,4,3,2,1,0:T(8,128)(2,1)S(1)} %pad_maximum_fusion.6), channel_id=1, source_target_pairs={{0,1},{1,0},{2,3},{3,2},{4,5},{5,4},{6,7},{7,6},{8,9},{9,8},{10,11... | collective-permute-start | bytes 2359304 | tf_op jit(solution)/shard_map/ppermute | solution.py:46
  34.9 3.4 %collective-permute-start.7 = (bf16[2,2,2,1,16,3072]{5,4,3,2,1,0:T(8,128)(2,1)S(1)}, bf16[2,2,2,1,16,3072]{5,4,3,2,1,0:T(8,128)(2,1)S(1)}, u32[]{:S(2)}, u32[]{:S(2)}) collective-permute-start(bf16[2,2,2,1,16,3072]{5,4,3,2,1,0:T(8,128)(2,1)S(1)} %pad_maximum_fusion.7), channel_id=1, source_target_pairs={{0,1},{1,0},{2,3},{3,2},{4,5},{5,4},{6,7},{7,6},{8,9},{9,8},{10,11... | collective-permute-start | bytes 2359304 | tf_op jit(solution)/shard_map/ppermute | solution.py:46
  38.4 10.5 %copy-start.5 = (bf16[2,2,2,2,16,3072]{5,4,3,2,1,0:T(8,128)(2,1)}, bf16[2,2,2,2,16,3072]{5,4,3,2,1,0:T(8,128)(2,1)S(1)}, u32[]{:S(2)}) copy-start(bf16[2,2,2,2,16,3072]{5,4,3,2,1,0:T(8,128)(2,1)S(1)} %pad_maximum_fusion.2) | copy-start | bytes 4718596
  38.4 10.5 %slice-start = ((s8[9437184]{0:T(1024)(128)(4,1)}), s8[4194304]{0:T(1024)(128)(4,1)S(1)}, s32[]{:S(2)}) async-start(s8[9437184]{0:T(1024)(128)(4,1)} %bitcast.58), calls=%async_computation | async-start | bytes 8388608
  56.8 6.6 %collective-permute-start.8 = (bf16[2,2,2,1,16,6144]{5,4,3,2,1,0:T(8,128)(2,1)}, bf16[2,2,2,1,16,6144]{5,4,3,2,1,0:T(8,128)(2,1)}, u32[]{:S(2)}, u32[]{:S(2)}) collective-permute-start(bf16[2,2,2,1,16,6144]{5,4,3,2,1,0:T(8,128)(2,1)} %slice.165), channel_id=1, source_target_pairs={{0,1},{1,0},{2,3},{3,2},{4,5},{5,4},{6,7},{7,6},{8,9},{9,8},{10,11... | collective-permute-start | bytes 4718600 | tf_op jit(solution)/shard_map/ppermute | solution.py:46
  66.6 4.0 %collective-permute-start.14 = (bf16[2,2,2,1,16,6144]{5,4,2,1,0,3:T(8,128)(2,1)S(1)}, bf16[2,2,2,1,16,6144]{5,4,2,1,0,3:T(8,128)(2,1)S(1)}, u32[]{:S(2)}, u32[]{:S(2)}) collective-permute-start(bf16[2,2,2,1,16,6144]{5,4,2,1,0,3:T(8,128)(2,1)S(1)} %copy.19), channel_id=1, source_target_pairs={{0,1},{1,0},{2,3},{3,2},{4,5},{5,4},{6,7},{7,6},{8,9},{9,8},{10,11... | collective-permute-start | bytes 4718600 | tf_op jit(solution)/shard_map/ppermute | solution.py:46
  69.2 19.6 %collective-permute-start.9 = (bf16[2,2,1,1,16,6144]{5,4,3,2,1,0:T(8,128)(2,1)S(1)}, bf16[2,2,1,1,16,6144]{5,4,3,2,1,0:T(8,128)(2,1)S(1)}, u32[]{:S(2)}, u32[]{:S(2)}) collective-permute-start(bf16[2,2,1,1,16,6144]{5,4,3,2,1,0:T(8,128)(2,1)S(1)} %slice.167), channel_id=1, source_target_pairs={{0,2},{1,3},{2,0},{3,1},{4,6},{5,7},{6,4},{7,5},{8,10},{9,11},{10,... | collective-permute-start | bytes 2359304 | tf_op jit(solution)/shard_map/ppermute | solution.py:46
  71.0 44.1 %copy-start.2 = (bf16[16,6144]{1,0:T(8,128)(2,1)S(1)}, bf16[16,6144]{1,0:T(8,128)(2,1)}, u32[]{:S(2)}) copy-start(bf16[16,6144]{1,0:T(8,128)(2,1)} %param.7) | copy-start | bytes 589828
  71.0 44.1 %copy-start.11 = (bf16[16,6144]{1,0:T(8,128)(2,1)S(1)}, bf16[16,6144]{1,0:T(8,128)(2,1)}, u32[]{:S(2)}) copy-start(bf16[16,6144]{1,0:T(8,128)(2,1)} %param.8) | copy-start | bytes 589828
  71.0 19.4 %collective-permute-start.15 = (bf16[2,1,2,1,16,6144]{5,4,2,1,0,3:T(8,128)(2,1)S(1)}, bf16[2,1,2,1,16,6144]{5,4,2,1,0,3:T(8,128)(2,1)S(1)}, u32[]{:S(2)}, u32[]{:S(2)}) collective-permute-start(bf16[2,1,2,1,16,6144]{5,4,2,1,0,3:T(8,128)(2,1)S(1)} %slice.166), channel_id=1, source_target_pairs={{0,4},{1,5},{2,6},{3,7},{4,0},{5,1},{6,2},{7,3},{8,12},{9,13},{10,... | collective-permute-start | bytes 2359304 | tf_op jit(solution)/shard_map/ppermute | solution.py:46
  89.1 10.4 %collective-permute-start.10 = (bf16[2,1,1,1,16,6144]{5,4,3,2,1,0:T(8,128)(2,1)S(1)}, bf16[2,1,1,1,16,6144]{5,4,3,2,1,0:T(8,128)(2,1)S(1)}, u32[]{:S(2)}, u32[]{:S(2)}) collective-permute-start(bf16[2,1,1,1,16,6144]{5,4,3,2,1,0:T(8,128)(2,1)S(1)} %slice.169), channel_id=1, source_target_pairs={{0,4},{1,5},{2,6},{3,7},{4,0},{5,1},{6,2},{7,3},{8,12},{9,13},{10,... | collective-permute-start | bytes 1179656 | tf_op jit(solution)/shard_map/ppermute | solution.py:46
  90.6 12.7 %collective-permute-start.16 = (bf16[2,1,1,1,16,6144]{5,4,2,1,0,3:T(8,128)(2,1)S(1)}, bf16[2,1,1,1,16,6144]{5,4,2,1,0,3:T(8,128)(2,1)S(1)}, u32[]{:S(2)}, u32[]{:S(2)}) collective-permute-start(bf16[2,1,1,1,16,6144]{5,4,2,1,0,3:T(8,128)(2,1)S(1)} %slice.168), channel_id=1, source_target_pairs={{0,2},{1,3},{2,0},{3,1},{4,6},{5,7},{6,4},{7,5},{8,10},{9,11},{10,... | collective-permute-start | bytes 1179656 | tf_op jit(solution)/shard_map/ppermute | solution.py:46
  99.5 15.6 %collective-permute-start.11 = (bf16[1,1,1,1,16,6144]{5,4,3,2,1,0:T(8,128)(2,1)S(1)}, bf16[1,1,1,1,16,6144]{5,4,3,2,1,0:T(8,128)(2,1)S(1)}, u32[]{:S(2)}, u32[]{:S(2)}) collective-permute-start(bf16[1,1,1,1,16,6144]{5,4,3,2,1,0:T(8,128)(2,1)S(1)} %slice.171), channel_id=1, source_target_pairs={{0,8},{1,9},{2,10},{3,11},{4,12},{5,13},{6,14},{7,15},{8,0},{9,1},... | collective-permute-start | bytes 589832 | tf_op jit(solution)/shard_map/ppermute | solution.py:46
  103.4 20.2 %collective-permute-start.17 = (bf16[1,1,1,1,16,6144]{5,4,2,1,0,3:T(8,128)(2,1)S(1)}, bf16[1,1,1,1,16,6144]{5,4,2,1,0,3:T(8,128)(2,1)S(1)}, u32[]{:S(2)}, u32[]{:S(2)}) collective-permute-start(bf16[1,1,1,1,16,6144]{5,4,2,1,0,3:T(8,128)(2,1)S(1)} %slice.170), channel_id=1, source_target_pairs={{0,8},{1,9},{2,10},{3,11},{4,12},{5,13},{6,14},{7,15},{8,0},{9,1},... | collective-permute-start | bytes 589832 | tf_op jit(solution)/shard_map/ppermute | solution.py:46
  115.2 16.7 %collective-permute-start.12 = (bf16[1,1,1,1,16,6144]{5,4,3,2,1,0:T(8,128)(2,1)S(1)}, bf16[1,1,1,1,16,6144]{5,4,3,2,1,0:T(8,128)(2,1)S(1)}, u32[]{:S(2)}, u32[]{:S(2)}) collective-permute-start(bf16[1,1,1,1,16,6144]{5,4,3,2,1,0:T(8,128)(2,1)S(1)} %fusion.24), channel_id=1, source_target_pairs={{0,8},{1,9},{2,10},{3,11},{4,12},{5,13},{6,14},{7,15},{8,0},{9,1},... | collective-permute-start | bytes 589832 | tf_op jit(solution)/shard_map/ppermute | solution.py:46
  123.6 12.5 %collective-permute-start.18 = (bf16[1,1,1,1,16,6144]{5,4,2,1,0,3:T(8,128)(2,1)S(1)}, bf16[1,1,1,1,16,6144]{5,4,2,1,0,3:T(8,128)(2,1)S(1)}, u32[]{:S(2)}, u32[]{:S(2)}) collective-permute-start(bf16[1,1,1,1,16,6144]{5,4,2,1,0,3:T(8,128)(2,1)S(1)} %multiply_convert_fusion.2), channel_id=1, source_target_pairs={{0,8},{1,9},{2,10},{3,11},{4,12},{5,13},{6,14},{7,15},{8,0},{9,1},... | collective-permute-start | bytes 589832 | tf_op jit(solution)/shard_map/ppermute | solution.py:46
  132.0 12.4 %collective-permute-start.13 = (bf16[2,1,1,1,16,6144]{5,4,3,2,1,0:T(8,128)(2,1)S(1)}, bf16[2,1,1,1,16,6144]{5,4,3,2,1,0:T(8,128)(2,1)S(1)}, u32[]{:S(2)}, u32[]{:S(2)}) collective-permute-start(bf16[2,1,1,1,16,6144]{5,4,3,2,1,0:T(8,128)(2,1)S(1)} %pad_maximum_fusion.13), channel_id=1, source_target_pairs={{0,4},{1,5},{2,6},{3,7},{4,0},{5,1},{6,2},{7,3},{8,12},{9,13},{10,... | collective-permute-start | bytes 1179656 | tf_op jit(solution)/shard_map/ppermute | solution.py:46
  136.2 10.9 %collective-permute-start.19 = (bf16[2,1,1,1,16,6144]{5,4,2,1,0,3:T(8,128)(2,1)S(1)}, bf16[2,1,1,1,16,6144]{5,4,2,1,0,3:T(8,128)(2,1)S(1)}, u32[]{:S(2)}, u32[]{:S(2)}) collective-permute-start(bf16[2,1,1,1,16,6144]{5,4,2,1,0,3:T(8,128)(2,1)S(1)} %pad_maximum_fusion.14), channel_id=1, source_target_pairs={{0,2},{1,3},{2,0},{3,1},{4,6},{5,7},{6,4},{7,5},{8,10},{9,11},{10,... | collective-permute-start | bytes 1179656 | tf_op jit(solution)/shard_map/ppermute | solution.py:46
  151.2 18.4 %collective-permute-start.20 = (bf16[2,2,1,1,16,6144]{5,4,3,2,1,0:T(8,128)(2,1)S(1)}, bf16[2,2,1,1,16,6144]{5,4,3,2,1,0:T(8,128)(2,1)S(1)}, u32[]{:S(2)}, u32[]{:S(2)}) collective-permute-start(bf16[2,2,1,1,16,6144]{5,4,3,2,1,0:T(8,128)(2,1)S(1)} %pad_maximum_fusion.8), channel_id=1, source_target_pairs={{0,2},{1,3},{2,0},{3,1},{4,6},{5,7},{6,4},{7,5},{8,10},{9,11},{10,... | collective-permute-start | bytes 2359304 | tf_op jit(solution)/shard_map/ppermute | solution.py:46
  152.8 18.2 %collective-permute-start.21 = (bf16[2,1,2,1,16,6144]{5,4,2,1,0,3:T(8,128)(2,1)S(1)}, bf16[2,1,2,1,16,6144]{5,4,2,1,0,3:T(8,128)(2,1)S(1)}, u32[]{:S(2)}, u32[]{:S(2)}) collective-permute-start(bf16[2,1,2,1,16,6144]{5,4,2,1,0,3:T(8,128)(2,1)S(1)} %pad_maximum_fusion.9), channel_id=1, source_target_pairs={{0,4},{1,5},{2,6},{3,7},{4,0},{5,1},{6,2},{7,3},{8,12},{9,13},{10,... | collective-permute-start | bytes 2359304 | tf_op jit(solution)/shard_map/ppermute | solution.py:46
  169.6 3.5 %collective-permute-start.22 = (bf16[2,2,2,1,16,6144]{5,4,3,2,1,0:T(8,128)(2,1)S(1)}, bf16[2,2,2,1,16,6144]{5,4,3,2,1,0:T(8,128)(2,1)S(1)}, u32[]{:S(2)}, u32[]{:S(2)}) collective-permute-start(bf16[2,2,2,1,16,6144]{5,4,3,2,1,0:T(8,128)(2,1)S(1)} %constant_dynamic-update-slice_fusion), channel_id=1, source_target_pairs={{0,1},{1,0},{2,3},{3,2},{4,5},{5,4},{6,7},{7,6},{8,9},{9,8},{10,11... | collective-permute-start | bytes 4718600 | tf_op jit(solution)/shard_map/ppermute | solution.py:46
  171.1 4.3 %collective-permute-start.23 = (bf16[2,2,2,1,16,6144]{5,4,2,1,0,3:T(8,128)(2,1)S(1)}, bf16[2,2,2,1,16,6144]{5,4,2,1,0,3:T(8,128)(2,1)S(1)}, u32[]{:S(2)}, u32[]{:S(2)}) collective-permute-start(bf16[2,2,2,1,16,6144]{5,4,2,1,0,3:T(8,128)(2,1)S(1)} %constant_dynamic-update-slice_fusion.2), channel_id=1, source_target_pairs={{0,1},{1,0},{2,3},{3,2},{4,5},{5,4},{6,7},{7,6},{8,9},{9,8},{10,11... | collective-permute-start | bytes 4718600 | tf_op jit(solution)/shard_map/ppermute | solution.py:46
  200.2 1.1 collective-permute-start.24
  212.3 3.5 %collective-permute-start.25 = (f32[1]{0:T(128)}, f32[1]{0:T(128)}, u32[]{:S(2)}, u32[]{:S(2)}) collective-permute-start(f32[1]{0:T(128)} %add.89), channel_id=1, source_target_pairs={{0,2},{1,3},{2,0},{3,1},{4,6},{5,7},{6,4},{7,5},{8,10},{9,11},{10,... | collective-permute-start | bytes 20 | tf_op jit(solution)/shard_map/ppermute | solution.py:46
  216.4 3.6 %collective-permute-start.26 = (f32[1]{0:T(128)}, f32[1]{0:T(128)}, u32[]{:S(2)}, u32[]{:S(2)}) collective-permute-start(f32[1]{0:T(128)} %add.90), channel_id=1, source_target_pairs={{0,4},{1,5},{2,6},{3,7},{4,0},{5,1},{6,2},{7,3},{8,12},{9,13},{10,... | collective-permute-start | bytes 20 | tf_op jit(solution)/shard_map/ppermute | solution.py:46
  220.6 4.5 %collective-permute-start.27 = (f32[1]{0:T(128)}, f32[1]{0:T(128)}, u32[]{:S(2)}, u32[]{:S(2)}) collective-permute-start(f32[1]{0:T(128)} %add.91), channel_id=1, source_target_pairs={{0,8},{1,9},{2,10},{3,11},{4,12},{5,13},{6,14},{7,15},{8,0},{9,1},... | collective-permute-start | bytes 20 | tf_op jit(solution)/shard_map/ppermute | solution.py:46
  (11 other events, 81.3 us)
